TPU v7x, 512 devices: a whole 4x8x8 slice. The times are simulated.
512 devices in a mesh: dp: 16 (over y_lo, x, core), mp: 32 (over y_hi, z).
Axes of the slice: x: 4, y: 8 (y_hi: 4, y_lo: 2; y = y_hi * 2 + y_lo), z: 8, core: 2. Of those that a mesh axis runs over, the one named last changes fastest.
Arguments:
- activations: bfloat16 [8192, 6144], P('dp', 'mp'), may hold values from -400 to 400
- ln_gain: bfloat16 [6144], P('mp'), may hold values from 0.099609375 to 1.8984375
- task_ids: int32 [32], P('dp'), may hold values from 0 to 7
- w_qkv: bfloat16 [6144, 32, 384], P(None, 'mp'), may hold values from -0.078125 to 0.078125
- a_shared: bfloat16 [256, 6144], P('dp', 'mp'), may hold values from -0.078125 to 0.078125
- b_shared: bfloat16 [32, 128, 256], P('mp'), may hold values from -0.375 to 0.375
- d_query: float32 [8, 256], replicated, may hold values from -4 to 4
- d_value: float32 [8, 256], replicated, may hold values from -4 to 4
- b_query: float32 [8, 32, 128], P(None, 'mp'), may hold values from -4 to 4
- b_value: float32 [8, 32, 128], P(None, 'mp'), may hold values from -4 to 4
Outputs:
- attended: bfloat16 [8192, 32, 128], P('dp', 'mp')
All inputs are finite; a program needn't handle non-finite values.
Results may differ from a plain program's by a relative error of at most 0.0087.
Values may be sent and summed in bfloat16 or wider, within the bound.
No kernel may reach another device: no remote copies, remote signals or barrier semaphores. Data moves between devices by JAX's collectives and lax.ppermute only.
A program may use at most 64 MiB of HBM per device.

v0:
```python
import jax
import jax.numpy as jnp
from jax import lax
from jax.sharding import PartitionSpec as P

eps = 1e-06


def unit_rows(values):
    centre = values - jnp.mean(values, axis=-1, keepdims=True)
    spread = jnp.mean(centre * centre, axis=-1, keepdims=True)
    return centre * lax.rsqrt(spread + eps)


def local(
    activations, ln_gain, task_ids, w_qkv, a_shared, b_shared, d_query, d_value, b_query, b_value
):
    tok_rows, local_width = activations.shape
    images = task_ids.shape[0]
    patches = tok_rows // images
    heads_here = w_qkv.shape[1]
    head_size = b_shared.shape[1]
    rank = b_shared.shape[2]
    tasks = d_query.shape[0]
    full_width = local_width * lax.axis_size("mp")
    values = activations.astype(jnp.float32)
    row_mean = lax.psum(jnp.sum(values, axis=1), "mp") / full_width
    centre = values - row_mean[:, None]
    row_var = lax.psum(jnp.sum(centre * centre, axis=1), "mp") / full_width
    local_norm = (centre * lax.rsqrt(row_var + eps)[:, None] * ln_gain.astype(jnp.float32)).astype(
        jnp.bfloat16
    )
    normed = lax.all_gather(local_norm, "mp", axis=1, tiled=True)
    proj_cols = heads_here * w_qkv.shape[2]
    qkv = jnp.dot(normed, w_qkv.reshape(full_width, proj_cols), preferred_element_type=jnp.float32)
    qkv = qkv.reshape(images, patches, heads_here, 3, head_size)
    contract = (((1,), (1,)), ((), ()))
    rank_block = lax.all_gather(a_shared, "dp", axis=0, tiled=True)
    ranks = lax.psum(
        lax.dot_general(local_norm, rank_block, contract, preferred_element_type=jnp.float32), "mp"
    )
    onehot = (task_ids[:, None] == lax.broadcasted_iota(jnp.int32, (images, tasks), 1)).astype(
        jnp.float32
    )
    highest = lax.Precision.HIGHEST
    dq_img = jnp.dot(onehot, d_query, precision=highest)
    dv_img = jnp.dot(onehot, d_value, precision=highest)
    bq_img = jnp.dot(onehot, b_query.reshape(tasks, heads_here * head_size), precision=highest)
    bv_img = jnp.dot(onehot, b_value.reshape(tasks, heads_here * head_size), precision=highest)
    ranks = ranks.reshape(images, patches, rank)
    scaled_q = (ranks * dq_img[:, None, :]).astype(jnp.bfloat16)
    scaled_v = (ranks * dv_img[:, None, :]).astype(jnp.bfloat16)
    stacked = jnp.concatenate(
        (scaled_q.reshape(tok_rows, rank), scaled_v.reshape(tok_rows, rank)), axis=0
    )
    lifted = lax.dot_general(
        stacked,
        b_shared.reshape(heads_here * head_size, rank),
        contract,
        preferred_element_type=jnp.float32,
    )
    up_q = lifted[:tok_rows].reshape(images, patches, heads_here, head_size)
    up_v = lifted[tok_rows:].reshape(images, patches, heads_here, head_size)
    query = qkv[:, :, :, 0, :] + up_q * bq_img.reshape(images, 1, heads_here, head_size)
    value = qkv[:, :, :, 2, :] + up_v * bv_img.reshape(images, 1, heads_here, head_size)
    query_unit = unit_rows(query).astype(jnp.bfloat16)
    key_unit = unit_rows(qkv[:, :, :, 1, :]).astype(jnp.bfloat16)
    value_bf = value.astype(jnp.bfloat16)
    scores = jnp.einsum("iphd,iqhd->ihpq", query_unit, key_unit, preferred_element_type=jnp.float32)
    scores = scores * (1.0 / jnp.sqrt(jnp.float32(head_size)))
    expo = jnp.exp(scores)
    probs = (expo / jnp.sum(expo, axis=-1, keepdims=True)).astype(jnp.bfloat16)
    result = jnp.einsum("ihpq,iqhd->iphd", probs, value_bf, preferred_element_type=jnp.float32)
    return result.astype(jnp.bfloat16).reshape(tok_rows, heads_here, head_size)


def solution(mesh):
    return jax.shard_map(
        local,
        mesh=mesh,
        in_specs=(
            P("dp", "mp"),
            P("mp"),
            P("dp"),
            P(None, "mp", None),
            P("dp", "mp"),
            P("mp", None, None),
            P(),
            P(),
            P(None, "mp", None),
            P(None, "mp", None),
        ),
        out_specs=P("dp", "mp", None),
        check_vma=False,
    )
```

profile of v0, /device:TPU:1, one launch (start us, length us, event | category | flops | bytes accessed | tf_op | source)
XLA Modules:
  0.0 646.3 jit_solution(14523547369636800500)
XLA Ops:
  6.5 0.0 copy-start
  6.6 0.0 all-reduce.2.cloned.1.call-start
  6.6 0.7 convert_element_type.50
  7.3 1.0 convert_reduce_fusion
  8.3 76.4 %psum.21 = f32[512]{0:T(512)S(1)} all-reduce(f32[512]{0:T(512)S(1)} %convert_reduce_fusion), channel_id=1, replica_groups=mesh['dp'=16,'mp'=32] {'mp'}, use_global_device_ids=true, to_apply=%region_1.0 | all-reduce | flops 512 | bytes 4096 | tf_op jit(solution)/shard_map/psum | solution.py:27
  84.7 1.0 fusion.10
  85.7 62.9 %psum.22 = f32[512]{0:T(512)S(1)} all-reduce(f32[512]{0:T(512)S(1)} %fusion.10), channel_id=1, replica_groups=mesh['dp'=16,'mp'=32] {'mp'}, use_global_device_ids=true, to_apply=%region_3.0 | all-reduce | flops 512 | bytes 4096 | tf_op jit(solution)/shard_map/psum | solution.py:29
  148.6 47.7 %all_gather.7 = bf16[256,192]{1,0:T(8,128)(2,1)S(1)} all-gather(bf16[16,192]{1,0:T(8,128)(2,1)} %param.14), channel_id=1, replica_groups=mesh['dp'=16,'mp'=32] {'dp'}, dimensions={0}, use_global_device_ids=true | all-gather | bytes 104448 | tf_op jit(solution)/shard_map/all_gather | solution.py:38
  196.4 1.0 fusion.12
  197.4 1.1 fusion.45
  198.5 0.0 all-reduce.2.cloned.1.call-update
  198.5 0.0 all-gather.2.cloned.1.call-start
  198.6 0.7 all-gather.2.cloned.1.call-update
  199.3 6.6 %copy.17 = bf16[6144,1,384]{0,2,1:T(8,128)(2,1)} copy(bf16[6144,1,384]{2,0,1:T(8,128)(2,1)} %param.13) | data formatting | bytes 9437184 | tf_op args[3]
  205.9 0.2 fusion.34
  206.1 0.2 fusion.35
  206.3 0.2 fusion.37
  206.5 0.2 fusion.36
  206.7 278.8 %all-reduce.2.cloned.1.call-done = f32[512,256]{1,0:T(8,128)} async-done(((f32[512,256]{1,0:T(8,128)}), f32[512,256]{1,0:T(8,128)}) %all-reduce.2.cloned.1.call-update) | async-done | bytes 524304 | tf_op jit(solution)/shard_map/psum | solution.py:39
  485.5 1.1 fusion.7
  486.6 0.3 fusion.2
  487.0 0.1 copy.18
  487.1 0.1 copy.20
  487.3 0.1 copy.19
  487.4 135.5 %all-gather.2.cloned.1.call-done = bf16[512,6144]{0,1:T(8,128)(2,1)} async-done(((bf16[512,192]{0,1:T(8,128)(2,1)}), bf16[512,6144]{0,1:T(8,128)(2,1)}) %all-gather.2.cloned.1.call-update) | async-done | bytes 6291472 | tf_op jit(solution)/shard_map/all_gather | solution.py:33
  622.9 8.7 %copy.16 = bf16[512,6144]{1,0:T(8,128)(2,1)} copy(bf16[512,6144]{0,1:T(8,128)(2,1)} %all-gather.2.cloned.1.call-done) | data formatting | bytes 12582912 | tf_op jit(solution)/shard_map/all_gather | solution.py:33
  631.6 6.2 convolution_bitcast_fusion
  637.8 0.1 fusion.32
  637.9 0.1 multiply_reduce_fusion
  638.1 0.3 fusion
  638.4 0.3 fusion.1
  638.7 0.8 copy.24
  (20 shorter events, 0.1 us)
Async XLA Ops:
  6.5 480.1 %copy-start = (bf16[1,128,256]{2,1,0:T(8,128)(2,1)S(1)}, bf16[1,128,256]{2,1,0:T(8,128)(2,1)}, u32[]{:S(2)}) copy-start(bf16[1,128,256]{2,1,0:T(8,128)(2,1)} %param.15) | copy-start | bytes 196612
  6.5 199.4 %copy-start.6 = (s32[2]{0:T(128)S(1)}, s32[2]{0:T(128)}, u32[]{:S(2)}) copy-start(s32[2]{0:T(128)} %param.12) | copy-start | bytes 28
  6.5 199.4 %copy-start.4 = (f32[8,1,128]{2,1,0:T(1,128)S(1)}, f32[8,1,128]{2,1,0:T(1,128)}, u32[]{:S(2)}) copy-start(f32[8,1,128]{2,1,0:T(1,128)} %param.18) | copy-start | bytes 12292
  6.5 199.6 %copy-start.5 = (f32[8,1,128]{2,1,0:T(1,128)S(1)}, f32[8,1,128]{2,1,0:T(1,128)}, u32[]{:S(2)}) copy-start(f32[8,1,128]{2,1,0:T(1,128)} %param.19) | copy-start | bytes 12292
  6.5 199.7 %copy-start.2 = (f32[8,256]{1,0:T(8,128)S(1)}, f32[8,256]{1,0:T(8,128)}, u32[]{:S(2)}) copy-start(f32[8,256]{1,0:T(8,128)} %param.16) | copy-start | bytes 24580
  6.5 199.9 %copy-start.3 = (f32[8,256]{1,0:T(8,128)S(1)}, f32[8,256]{1,0:T(8,128)}, u32[]{:S(2)}) copy-start(f32[8,256]{1,0:T(8,128)} %param.17) | copy-start | bytes 24580
  6.6 478.9 %all-reduce.2.cloned.1.call-start = ((), (), s32[]{:S(2)}) async-start(), calls=%async_computation.1 | async-start | bytes 1048576 | tf_op jit(solution)/shard_map/psum | solution.py:39
  197.4 1.2 copy-start.1
  198.5 424.4 %all-gather.2.cloned.1.call-start = ((), (), s32[]{:S(2)}) async-start(), calls=%async_computation | async-start | bytes 6488064 | tf_op jit(solution)/shard_map/all_gather | solution.py:33
Sparse Core Ops, SparseCore 0:
  198.6 286.8 all-reduce.1
  489.1 133.7 all-gather.1
where the time goes:
time: 650 us; the launch traced here: 646 us
  waiting for transfers between devices  415 us (64%)
  blocking collectives  187 us (29%)
  local copies, waits for them, and re-layouts  16.6 us (3%)
  between operations  13.5 us (2%)
  matrix products  8.89 us (1%)
    psum x1, waiting for transfers between devices, local(): lax.psum(lax.dot_general(local_norm, rank_block, contract, preferred_elem...  279 us
    all_gather x1, waiting for transfers between devices, local(): normed = lax.all_gather(local_norm, 'mp', axis=1, tiled=True)  136 us
    psum x1, blocking collectives, local(): row_mean = lax.psum(jnp.sum(values, axis=1), 'mp') / full_width  76.4 us
    psum x1, blocking collectives, local(): row_var = lax.psum(jnp.sum(centre * centre, axis=1), 'mp') / full_width  62.9 us
    all_gather x1, blocking collectives, local(): rank_block = lax.all_gather(a_shared, 'dp', axis=0, tiled=True)  47.7 us
  transfers between devices with their start and end apart: 2, of which 2 were waited for; matrix products, arithmetic and copies ran while one was open for 1% of the time, Pallas kernels for 0%

commit v1 on v0

v1 whole, which is shorter than its diff:
```python
import jax
import jax.numpy as jnp
from jax import lax
from jax.experimental import pallas as pl
from jax.experimental.pallas import tpu as pltpu
from jax.sharding import PartitionSpec as P

eps = 1e-06
N_Y, N_Z = 4, 8
along_y = [[y * N_Z + z for y in range(N_Y)] for z in range(N_Z)]
along_z = [[y * N_Z + z for z in range(N_Z)] for y in range(N_Y)]


def unit_columns(values):
    centre = values - jnp.mean(values, axis=0, keepdims=True)
    spread = jnp.mean(centre * centre, axis=0, keepdims=True)
    return (centre * lax.rsqrt(spread + eps)).astype(jnp.bfloat16)


def heads_kernel(x_ref, w_ref, gain_ref, stat_ref, low_ref, b_ref, scale_ref, out_ref, acc_ref):
    step = pl.program_id(0)

    @pl.when(step == 0)
    def _():
        acc_ref[...] = jnp.zeros_like(acc_ref)

    gain = jnp.transpose(gain_ref[0])[:, :1]
    centre = x_ref[...].astype(jnp.float32) - stat_ref[0:1, :]
    normed = (centre * stat_ref[1:2, :] * gain).astype(jnp.bfloat16)
    acc_ref[...] += jnp.dot(w_ref[0], normed, preferred_element_type=jnp.float32)

    @pl.when(step == pl.num_programs(0) - 1)
    def _():
        size = b_ref.shape[0]
        images = scale_ref.shape[1] // 2
        patches = x_ref.shape[1] // images
        rank = b_ref.shape[1]
        up_q = jnp.dot(b_ref[...], low_ref[:rank], preferred_element_type=jnp.float32)
        up_v = jnp.dot(b_ref[...], low_ref[rank:], preferred_element_type=jnp.float32)
        for i in range(images):
            cols = slice(i * patches, (i + 1) * patches)
            query = acc_ref[:size, cols] + up_q[:, cols] * scale_ref[:, i : i + 1]
            value = (
                acc_ref[2 * size :, cols] + up_v[:, cols] * scale_ref[:, images + i : images + i + 1]
            ).astype(jnp.bfloat16)
            query = unit_columns(query)
            key = unit_columns(acc_ref[size : 2 * size, cols])
            scores = lax.dot_general(
                key, query, (((0,), (0,)), ((), ())), preferred_element_type=jnp.float32
            )
            expo = jnp.exp(scores * (1.0 / jnp.sqrt(jnp.float32(size))))
            probs = (expo / jnp.sum(expo, axis=0, keepdims=True)).astype(jnp.bfloat16)
            mixed = jnp.dot(value, probs, preferred_element_type=jnp.float32)
            out_ref[cols, :] = jnp.transpose(mixed).astype(out_ref.dtype)


def local(
    activations, ln_gain, task_ids, w_qkv, a_shared, b_shared, d_query, d_value, b_query, b_value
):
    rows, width = activations.shape
    images = task_ids.shape[0]
    patches = rows // images
    size = b_shared.shape[1]
    rank = b_shared.shape[2]
    tasks = d_query.shape[0]
    parts = lax.axis_size("mp")
    full = width * parts
    own = rank // parts

    flat = activations.T
    by_y = lax.all_gather(flat, "mp", axis=0, tiled=True, axis_index_groups=along_y)
    whole = lax.all_gather(by_y, "mp", axis=0, tiled=True, axis_index_groups=along_z)

    gain = ln_gain.astype(jnp.float32)
    down = lax.all_gather(a_shared, "dp", axis=0, tiled=True)
    values = flat.astype(jnp.float32)
    mean_here = jnp.mean(values, axis=0)
    centre = values - mean_here
    square_here = jnp.sum(centre * centre, axis=0)
    partial = jnp.dot(
        down, (centre * gain[:, None]).astype(jnp.bfloat16), preferred_element_type=jnp.float32
    )
    down_gain = jnp.sum(down.astype(jnp.float32) * gain, axis=1)
    extra = jnp.concatenate(
        (
            jnp.broadcast_to(mean_here, (parts, 1, rows)),
            jnp.broadcast_to(square_here, (parts, 1, rows)),
            jnp.concatenate(
                (
                    jnp.broadcast_to(gain, (parts, 1, width)),
                    down_gain.reshape(parts, 1, own),
                    jnp.zeros((parts, 1, rows - width - own), jnp.float32),
                ),
                axis=2,
            ),
        ),
        axis=1,
    )
    sent = jnp.concatenate((partial.reshape(parts, own, rows), extra), axis=1)
    came = lax.all_to_all(sent, "mp", 0, 0)
    means = came[:, own]
    row_mean = jnp.mean(means, axis=0)
    offset = means - row_mean
    row_var = (jnp.sum(came[:, own + 1], axis=0) + width * jnp.sum(offset * offset, axis=0)) / full
    row_scale = lax.rsqrt(row_var + eps)
    gains = came[:, own + 2, :width]
    ranks = jnp.sum(
        came[:, :own] + came[:, own + 2, width : width + own, None] * offset[:, None, :], axis=0
    )
    ranks = ranks * row_scale

    onehot = (task_ids[:, None] == lax.broadcasted_iota(jnp.int32, (images, tasks), 1)).astype(
        jnp.float32
    )
    highest = lax.Precision.HIGHEST
    at = lax.axis_index("mp") * own
    dq = jnp.dot(onehot, lax.dynamic_slice_in_dim(d_query, at, own, 1), precision=highest)
    dv = jnp.dot(onehot, lax.dynamic_slice_in_dim(d_value, at, own, 1), precision=highest)
    by_image = ranks.reshape(own, images, patches)
    scaled = jnp.stack((by_image * dq.T[:, :, None], by_image * dv.T[:, :, None]), axis=0)
    scaled = scaled.reshape(1, 2 * own, rows).astype(jnp.bfloat16)
    low = lax.all_to_all(jnp.broadcast_to(scaled, (parts, 2 * own, rows)), "mp", 0, 0)
    low = low.reshape(parts, 2, own, rows).transpose(1, 0, 2, 3).reshape(2 * rank, rows)

    bq = jnp.dot(onehot, b_query.reshape(tasks, size), precision=highest)
    bv = jnp.dot(onehot, b_value.reshape(tasks, size), precision=highest)
    scale = jnp.concatenate((bq, bv), axis=0).T
    stat = jnp.stack((row_mean, row_scale), axis=0)
    block = N_Y * width
    outs = w_qkv.shape[2]
    weights = (
        w_qkv.reshape(N_Y, N_Z, width, outs).transpose(1, 3, 0, 2).reshape(N_Z, outs, block)
    )
    gains = gains.reshape(N_Y, N_Z, width).transpose(1, 0, 2).reshape(N_Z, 1, block)
    gains = jnp.broadcast_to(gains, (N_Z, 8, block))

    result = pl.pallas_call(
        heads_kernel,
        grid=(N_Z,),
        in_specs=[
            pl.BlockSpec((block, rows), lambda i: (i, 0)),
            pl.BlockSpec((1, outs, block), lambda i: (i, 0, 0)),
            pl.BlockSpec((1, 8, block), lambda i: (i, 0, 0)),
            pl.BlockSpec((2, rows), lambda i: (0, 0)),
            pl.BlockSpec((2 * rank, rows), lambda i: (0, 0)),
            pl.BlockSpec((size, rank), lambda i: (0, 0)),
            pl.BlockSpec((size, 2 * images), lambda i: (0, 0)),
        ],
        out_specs=pl.BlockSpec((rows, size), lambda i: (0, 0)),
        out_shape=jax.ShapeDtypeStruct((rows, size), jnp.bfloat16),
        scratch_shapes=[pltpu.VMEM((outs, rows), jnp.float32)],
        compiler_params=pltpu.CompilerParams(
            dimension_semantics=("arbitrary",), vmem_limit_bytes=40 * 2**20
        ),
        cost_estimate=pl.CostEstimate(
            flops=2 * full * outs * rows, bytes_accessed=12 * 2**20, transcendentals=0
        ),
        name="heads",
    )(whole, weights, gains, stat, low, b_shared.reshape(size, rank), scale)
    return result.reshape(rows, 1, size)


def solution(mesh):
    return jax.shard_map(
        local,
        mesh=mesh,
        in_specs=(
            P("dp", "mp"),
            P("mp"),
            P("dp"),
            P(None, "mp", None),
            P("dp", "mp"),
            P("mp", None, None),
            P(),
            P(),
            P(None, "mp", None),
            P(None, "mp", None),
        ),
        out_specs=P("dp", "mp", None),
        check_vma=False,
    )
```

time: 650 us -> 170 us (0.26)
  waiting for transfers between devices: 415 us -> 62.5 us
  blocking collectives: 187 us -> 43.1 us
  starting transfers between devices: 0.08 us -> 16.8 us
  Pallas kernels: 0 us -> 8.43 us
  matrix products: 8.89 us -> 1.95 us
    psum x1 -> x0, waiting for transfers between devices: 279 us -> none  [local(): lax.psum(lax.dot_general(local_norm, rank_block, contract, preferred_elem...]
    psum x2 -> x0, blocking collectives: 139 us -> none  [the longest x1 76.4 us: local(): row_mean = lax.psum(jnp.sum(values, axis=1), 'mp') / full_width]
    all_gather x1, waiting for transfers between devices: 136 us -> 24.4 us  [local(): lax.all_gather(by_y, 'mp', axis=0, tiled=True, axis_index_groups=along_z)]
    all_to_all x0 -> x2, waiting for transfers between devices: none -> 38.2 us  [the longest x1 35.2 us: local(): came = lax.all_to_all(sent, 'mp', 0, 0)]
    all_to_all x0 -> x2, starting transfers between devices: none -> 16.8 us  [the longest x1 11.9 us: local(): came = lax.all_to_all(sent, 'mp', 0, 0)]
    all_gather x1 -> x0, local copies, waits for them, and re-layouts: 8.7 us -> none  [local(): normed = lax.all_gather(local_norm, 'mp', axis=1, tiled=True)]
    pallas_call x0 -> x1, Pallas kernels: none -> 8.43 us  [local(): pl.pallas_call(heads_kernel, grid=(N_Z,), in_specs=[pl.BlockSpec((block,...]
    dot_general x9 -> x5, matrix products: 8.89 us -> 1.95 us  [the longest x1 1.2 us: local(): jnp.dot(down, (centre * gain[:, None]).astype(jnp.bfloat16), preferred_el...]
  transfers between devices with their start and end apart: 2 -> 3, of which waited for: 2 -> 3; matrix products, arithmetic and copies ran while one was open for 1% -> 12% of each run, Pallas kernels for 0% -> 0%
where the time goes in v1:
time: 170 us; the launch traced here: 169 us
  waiting for transfers between devices  62.5 us (37%)
  blocking collectives  43.1 us (25%)
  local copies, waits for them, and re-layouts  18.5 us (11%)
  starting transfers between devices  16.8 us (10%)
  between operations  13.6 us (8%)
  Pallas kernels  8.43 us (5%)
  other arithmetic  4.44 us (3%)
  matrix products  1.95 us (1%)
    all_to_all x1, waiting for transfers between devices, local(): came = lax.all_to_all(sent, 'mp', 0, 0)  35.2 us
    all_gather x1, waiting for transfers between devices, local(): lax.all_gather(by_y, 'mp', axis=0, tiled=True, axis_index_groups=along_z)  24.4 us
    all_gather x1, blocking collectives, local(): down = lax.all_gather(a_shared, 'dp', axis=0, tiled=True)  22.3 us
    all_gather x1, blocking collectives, local(): lax.all_gather(flat, 'mp', axis=0, tiled=True, axis_index_groups=along_y)  20.7 us
    all_to_all x1, starting transfers between devices, local(): came = lax.all_to_all(sent, 'mp', 0, 0)  11.9 us
    pallas_call x1, Pallas kernels, local(): pl.pallas_call(heads_kernel, grid=(N_Z,), in_specs=[pl.BlockSpec((block,...  8.43 us
    reshape x1, local copies, waits for them, and re-layouts, local(): w_qkv.reshape(N_Y, N_Z, width, outs).transpose(1, 3, 0, 2)  6.69 us
    transpose x1, local copies, waits for them, and re-layouts, local(): w_qkv.reshape(N_Y, N_Z, width, outs).transpose(1, 3, 0, 2)  5.16 us
  transfers between devices with their start and end apart: 3, of which 3 were waited for; matrix products, arithmetic and copies ran while one was open for 12% of the time, Pallas kernels for 0%

profile of v1, /device:TPU:1, one launch (start us, length us, event | category | flops | bytes accessed | tf_op | source)
XLA Modules:
  0.0 169.3 jit_solution(5628231670624297615)
XLA Ops:
  6.5 20.7 %all_gather.9 = bf16[768,512]{1,0:T(8,128)(2,1)} all-gather(bf16[192,512]{1,0:T(8,128)(2,1)} %bitcast.54), channel_id=1, replica_groups={{0,8,16,24},{1,9,17,25},{2,10,18,26},{3,11,19,27},{4,12,20,28},{5,13,21..., dimensions={0}, use_global_device_ids=true | all-gather | bytes 983040 | tf_op jit(solution)/shard_map/all_gather | solution.py:71
  27.3 0.7 convert_element_type.23
  28.0 22.3 %all_gather.11 = bf16[256,192]{1,0:T(8,128)(2,1)S(1)} all-gather(bf16[16,192]{1,0:T(8,128)(2,1)} %param.14), channel_id=1, replica_groups=mesh['dp'=16,'mp'=32] {'dp'}, dimensions={0}, use_global_device_ids=true | all-gather | bytes 104448 | tf_op jit(solution)/shard_map/all_gather | solution.py:75
  50.3 0.1 multiply_reduce_fusion
  50.4 0.1 reshape.144
  50.5 0.1 pad.11.clone
  50.6 1.0 convert_reduce_fusion
  51.6 1.0 fusion.4
  52.6 1.2 convolution_bitcast_fusion
  53.9 1.2 maximum_maximum_fusion
  55.1 11.9 %all-to-all-start = ((f32[32,11,512]{2,1,0:T(8,128)}), f32[32,11,512]{2,1,0:T(8,128)S(1)}, u32[]{:S(2)}, u32[]{:S(2)}) async-start(f32[32,11,512]{2,1,0:T(8,128)} %maximum_maximum_fusion), calls=%async_computation | async-start | bytes 2097152 | tf_op jit(solution)/shard_map/all_to_all | solution.py:100
  67.0 0.2 fusion.10
  67.2 0.2 fusion.12
  67.4 35.2 %all-to-all-done = f32[32,11,512]{2,1,0:T(8,128)S(1)} async-done(((f32[32,11,512]{2,1,0:T(8,128)}), f32[32,11,512]{2,1,0:T(8,128)S(1)}, u32[]{:S(2)}, u32[]{:S(2)}) %all-to-all-start) | async-done | bytes 720928 | tf_op jit(solution)/shard_map/all_to_all | solution.py:100
  102.6 0.1 slice_reduce_fusion.1
  102.7 0.1 broadcast_subtract_fusion
  102.9 0.1 slice.24
  103.0 0.1 fusion
  103.1 0.1 multiply_convert_fusion.1
  103.2 0.9 broadcast_in_dim.39
  104.1 4.9 %all-to-all-start.1 = ((bf16[32,16,512]{2,1,0:T(8,128)(2,1)}), bf16[32,16,512]{2,1,0:T(8,128)(2,1)S(1)}, u32[]{:S(2)}, u32[]{:S(2)}) async-start(bf16[32,16,512]{2,1,0:T(8,128)(2,1)} %broadcast_in_dim.39), calls=%async_computation.1 | async-start | bytes 1048576 | tf_op jit(solution)/shard_map/all_to_all | solution.py:122
  109.0 5.2 %copy.28 = bf16[8,384,4,192]{1,3,2,0:T(8,128)(2,1)} copy(bf16[8,384,4,192]{1,3,0,2:T(8,128)(2,1)} %bitcast.53) | data formatting | bytes 9437184 | tf_op jit(solution)/shard_map/transpose | solution.py:132
  114.1 6.7 %copy.33.w_ref = bf16[8,384,768]{2,1,0:T(8,128)(2,1)} copy(bf16[8,384,768]{1,2,0:T(8,128)(2,1)} %bitcast.52) | data formatting | bytes 9437184 | tf_op jit(solution)/shard_map/reshape | solution.py:132
  120.8 0.2 fusion.14
  121.0 0.2 fusion.15
  121.2 0.1 copy.32
  121.4 0.1 broadcast_in_dim.18
  121.5 2.9 %all-to-all-done.1 = bf16[32,16,512]{2,1,0:T(8,128)(2,1)S(1)} async-done(((bf16[32,16,512]{2,1,0:T(8,128)(2,1)}), bf16[32,16,512]{2,1,0:T(8,128)(2,1)S(1)}, u32[]{:S(2)}, u32[]{:S(2)}) %all-to-all-start.1) | async-done | bytes 524320 | tf_op jit(solution)/shard_map/all_to_all | solution.py:122
  124.5 24.4 %all-gather.2.cloned.1.call-done.x_ref = bf16[6144,512]{1,0:T(8,128)(2,1)} async-done(((bf16[768,512]{1,0:T(8,128)(2,1)}), bf16[6144,512]{1,0:T(8,128)(2,1)}) %all-gather.2.cloned.1.call-update) | async-done | bytes 6291472 | tf_op jit(solution)/shard_map/all_gather | solution.py:72
  148.9 2.3 %copy-done.1 = bf16[8,384,768]{2,1,0:T(8,128)(2,1)S(1)} copy-done((bf16[8,384,768]{2,1,0:T(8,128)(2,1)S(1)}, bf16[8,384,768]{2,1,0:T(8,128)(2,1)}, u32[]{:S(2)}) %copy-start.1) | copy-done | bytes 4718616
  151.2 2.8 %copy-done.2 = bf16[6144,512]{1,0:T(8,128)(2,1)S(1)} copy-done((bf16[6144,512]{1,0:T(8,128)(2,1)S(1)}, bf16[6144,512]{1,0:T(8,128)(2,1)}, u32[]{:S(2)}) %copy-start.2) | copy-done | bytes 6291480
  154.0 8.4 %heads.1 = bf16[512,128]{1,0:T(8,128)(2,1)} custom-call(bf16[6144,512]{1,0:T(8,128)(2,1)S(1)} %copy-done.2, bf16[8,384,768]{2,1,0:T(8,128)(2,1)S(1)} %copy-done.1, f32[8,8,768]{2,1,0:T(8,128)S(1)} %broadcast_in_dim.38.gain_ref, f32[2,512]{1,0:T(2,128)S(1)} %pad_maximum_fusion.1.stat_ref, bf16[512,512]{1,0:T(8,128)(2,1)S(1)} %bitcast.49, ...), custom_call_target="tpu_custom_call" | custom-call | flops 2415919104 | bytes 12582912 | tf_op jit(solution)/shard_map/heads/pallas_call | solution.py:137
  (34 shorter events, 0.3 us)
Async XLA Ops:
  6.5 60.5 %copy-start = (f32[8,256]{1,0:T(8,128)S(1)}, f32[8,256]{1,0:T(8,128)}, u32[]{:S(2)}) copy-start(f32[8,256]{1,0:T(8,128)} %param.17) | copy-start | bytes 24580
  6.5 60.5 %copy-start.7 = (s32[2]{0:T(128)S(1)}, s32[2]{0:T(128)}, u32[]{:S(2)}) copy-start(s32[2]{0:T(128)} %param.12) | copy-start | bytes 28
  6.5 60.7 %copy-start.4 = (f32[8,256]{1,0:T(8,128)S(1)}, f32[8,256]{1,0:T(8,128)}, u32[]{:S(2)}) copy-start(f32[8,256]{1,0:T(8,128)} %param.16) | copy-start | bytes 24580
  6.5 142.3 %all-gather.2.cloned.1.call-start = ((), (), s32[]{:S(2)}) async-start(), calls=%async_computation.2 | async-start | bytes 7077888 | tf_op jit(solution)/shard_map/all_gather | solution.py:72
  55.1 47.5 %all-to-all-start = ((f32[32,11,512]{2,1,0:T(8,128)}), f32[32,11,512]{2,1,0:T(8,128)S(1)}, u32[]{:S(2)}, u32[]{:S(2)}) async-start(f32[32,11,512]{2,1,0:T(8,128)} %maximum_maximum_fusion), calls=%async_computation | async-start | bytes 2097152 | tf_op jit(solution)/shard_map/all_to_all | solution.py:100
  104.1 20.4 %all-to-all-start.1 = ((bf16[32,16,512]{2,1,0:T(8,128)(2,1)}), bf16[32,16,512]{2,1,0:T(8,128)(2,1)S(1)}, u32[]{:S(2)}, u32[]{:S(2)}) async-start(bf16[32,16,512]{2,1,0:T(8,128)(2,1)} %broadcast_in_dim.39), calls=%async_computation.1 | async-start | bytes 1048576 | tf_op jit(solution)/shard_map/all_to_all | solution.py:122
  114.1 6.7 %copy-start.5 = (f32[8,1,128]{2,1,0:T(1,128)S(1)}, f32[8,1,128]{2,1,0:T(1,128)}, u32[]{:S(2)}) copy-start(f32[8,1,128]{2,1,0:T(1,128)} %param.19) | copy-start | bytes 12292
  114.1 6.9 %copy-start.6 = (f32[8,1,128]{2,1,0:T(1,128)S(1)}, f32[8,1,128]{2,1,0:T(1,128)}, u32[]{:S(2)}) copy-start(f32[8,1,128]{2,1,0:T(1,128)} %param.18) | copy-start | bytes 12292
  114.1 34.7 %copy-start.3 = (bf16[1,128,256]{2,1,0:T(8,128)(2,1)S(1)}, bf16[1,128,256]{2,1,0:T(8,128)(2,1)}, u32[]{:S(2)}) copy-start(bf16[1,128,256]{2,1,0:T(8,128)(2,1)} %param.15) | copy-start | bytes 196612
  148.9 2.3 %copy-start.1 = (bf16[8,384,768]{2,1,0:T(8,128)(2,1)S(1)}, bf16[8,384,768]{2,1,0:T(8,128)(2,1)}, u32[]{:S(2)}) copy-start(bf16[8,384,768]{2,1,0:T(8,128)(2,1)} %copy.33.w_ref) | copy-start | bytes 14155780
  151.2 2.8 %copy-start.2 = (bf16[6144,512]{1,0:T(8,128)(2,1)S(1)}, bf16[6144,512]{1,0:T(8,128)(2,1)}, u32[]{:S(2)}) copy-start(bf16[6144,512]{1,0:T(8,128)(2,1)} %all-gather.2.cloned.1.call-done.x_ref) | copy-start | bytes 18874372
Sparse Core Ops, SparseCore 0:
  27.4 121.3 all-gather.1

commit v2 on v1

--- a/solution.py
+++ b/solution.py
@@ -9,6 +9,13 @@
 N_Y, N_Z = 4, 8
 along_y = [[y * N_Z + z for y in range(N_Y)] for z in range(N_Z)]
 along_z = [[y * N_Z + z for z in range(N_Z)] for y in range(N_Y)]
+
+
+def terms(values):
+    high = lax.reduce_precision(values, 8, 7)
+    rest = values - high
+    middle = lax.reduce_precision(rest, 8, 7)
+    return [part.astype(jnp.bfloat16) for part in (high, middle, rest - middle)]
 
 
 def unit_columns(values):
@@ -66,48 +73,64 @@
     parts = lax.axis_size("mp")
     full = width * parts
     own = rank // parts
+    groups = lax.axis_size("dp")
 
     flat = activations.T
     by_y = lax.all_gather(flat, "mp", axis=0, tiled=True, axis_index_groups=along_y)
     whole = lax.all_gather(by_y, "mp", axis=0, tiled=True, axis_index_groups=along_z)
 
-    gain = ln_gain.astype(jnp.float32)
-    down = lax.all_gather(a_shared, "dp", axis=0, tiled=True)
-    values = flat.astype(jnp.float32)
+    block = N_Y * width
+    quarter = rank // N_Y
+    down = lax.all_to_all(jnp.broadcast_to(a_shared, (groups, rank // groups, width)), "dp", 0, 0)
+    down = jnp.concatenate(
+        (
+            down.reshape(N_Y, quarter, width),
+            jnp.broadcast_to(ln_gain, (N_Y, 1, width)),
+            jnp.zeros((N_Y, 15, width), jnp.bfloat16),
+        ),
+        axis=1,
+    )
+    down = lax.all_to_all(down, "mp", 0, 0, axis_index_groups=along_y)
+    gain = down[:, quarter].reshape(block)
+    down = down[:, :quarter].transpose(1, 0, 2).reshape(quarter, block)
+    values = by_y.astype(jnp.float32)
     mean_here = jnp.mean(values, axis=0)
     centre = values - mean_here
     square_here = jnp.sum(centre * centre, axis=0)
+    gain_here = gain.astype(jnp.float32)
     partial = jnp.dot(
-        down, (centre * gain[:, None]).astype(jnp.bfloat16), preferred_element_type=jnp.float32
-    )
-    down_gain = jnp.sum(down.astype(jnp.float32) * gain, axis=1)
-    extra = jnp.concatenate(
+        down, (centre * gain_here[:, None]).astype(jnp.bfloat16), preferred_element_type=jnp.float32
+    )
+    down_gain = jnp.sum(down.astype(jnp.float32) * gain_here, axis=1).reshape(N_Z, own)
+    lead = rows - (block - rows)
+    last = jnp.concatenate(
         (
-            jnp.broadcast_to(mean_here, (parts, 1, rows)),
-            jnp.broadcast_to(square_here, (parts, 1, rows)),
-            jnp.concatenate(
-                (
-                    jnp.broadcast_to(gain, (parts, 1, width)),
-                    down_gain.reshape(parts, 1, own),
-                    jnp.zeros((parts, 1, rows - width - own), jnp.float32),
-                ),
-                axis=2,
-            ),
+            *terms(down_gain),
+            jnp.zeros((N_Z, lead - 3 * own), jnp.bfloat16),
+            jnp.broadcast_to(gain, (N_Z, block)),
         ),
         axis=1,
     )
-    sent = jnp.concatenate((partial.reshape(parts, own, rows), extra), axis=1)
-    came = lax.all_to_all(sent, "mp", 0, 0)
-    means = came[:, own]
+    stats = jnp.stack(terms(mean_here) + terms(square_here), axis=0)
+    sent = jnp.concatenate(
+        (
+            partial.astype(jnp.bfloat16).reshape(N_Z, own, rows),
+            jnp.broadcast_to(stats, (N_Z, 6, rows)),
+            last.reshape(N_Z, 2, rows),
+        ),
+        axis=1,
+    )
+    came = lax.all_to_all(sent, "mp", 0, 0, axis_index_groups=along_z).astype(jnp.float32)
+    means = came[:, own] + came[:, own + 1] + came[:, own + 2]
+    squares = came[:, own + 3] + came[:, own + 4] + came[:, own + 5]
+    side = came[:, own + 6 :].reshape(N_Z, 2 * rows)
+    gains = side[:, lead:]
+    down_gains = side[:, :own] + side[:, own : 2 * own] + side[:, 2 * own : 3 * own]
     row_mean = jnp.mean(means, axis=0)
     offset = means - row_mean
-    row_var = (jnp.sum(came[:, own + 1], axis=0) + width * jnp.sum(offset * offset, axis=0)) / full
+    row_var = (jnp.sum(squares, axis=0) + block * jnp.sum(offset * offset, axis=0)) / full
     row_scale = lax.rsqrt(row_var + eps)
-    gains = came[:, own + 2, :width]
-    ranks = jnp.sum(
-        came[:, :own] + came[:, own + 2, width : width + own, None] * offset[:, None, :], axis=0
-    )
-    ranks = ranks * row_scale
+    ranks = jnp.sum(came[:, :own] + down_gains[:, :, None] * offset[:, None, :], axis=0) * row_scale
 
     onehot = (task_ids[:, None] == lax.broadcasted_iota(jnp.int32, (images, tasks), 1)).astype(
         jnp.float32
@@ -118,20 +141,24 @@
     dv = jnp.dot(onehot, lax.dynamic_slice_in_dim(d_value, at, own, 1), precision=highest)
     by_image = ranks.reshape(own, images, patches)
     scaled = jnp.stack((by_image * dq.T[:, :, None], by_image * dv.T[:, :, None]), axis=0)
-    scaled = scaled.reshape(1, 2 * own, rows).astype(jnp.bfloat16)
-    low = lax.all_to_all(jnp.broadcast_to(scaled, (parts, 2 * own, rows)), "mp", 0, 0)
+    scaled = scaled.reshape(2 * own, rows).astype(jnp.bfloat16)
+    low = lax.all_to_all(
+        jnp.broadcast_to(scaled, (N_Z, 2 * own, rows)), "mp", 0, 0, axis_index_groups=along_z
+    )
+    low = lax.all_to_all(
+        jnp.broadcast_to(low, (N_Y, N_Z, 2 * own, rows)), "mp", 0, 0, axis_index_groups=along_y
+    )
     low = low.reshape(parts, 2, own, rows).transpose(1, 0, 2, 3).reshape(2 * rank, rows)
 
     bq = jnp.dot(onehot, b_query.reshape(tasks, size), precision=highest)
     bv = jnp.dot(onehot, b_value.reshape(tasks, size), precision=highest)
     scale = jnp.concatenate((bq, bv), axis=0).T
     stat = jnp.stack((row_mean, row_scale), axis=0)
-    block = N_Y * width
     outs = w_qkv.shape[2]
     weights = (
         w_qkv.reshape(N_Y, N_Z, width, outs).transpose(1, 3, 0, 2).reshape(N_Z, outs, block)
     )
-    gains = gains.reshape(N_Y, N_Z, width).transpose(1, 0, 2).reshape(N_Z, 1, block)
+    gains = gains.reshape(N_Z, 1, block)
     gains = jnp.broadcast_to(gains, (N_Z, 8, block))
 
     result = pl.pallas_call(
@@ -150,7 +177,7 @@
         out_shape=jax.ShapeDtypeStruct((rows, size), jnp.bfloat16),
         scratch_shapes=[pltpu.VMEM((outs, rows), jnp.float32)],
         compiler_params=pltpu.CompilerParams(
-            dimension_semantics=("arbitrary",), vmem_limit_bytes=40 * 2**20
+            dimension_semantics=("arbitrary",), vmem_limit_bytes=56 * 2**20
         ),
         cost_estimate=pl.CostEstimate(
             flops=2 * full * outs * rows, bytes_accessed=12 * 2**20, transcendentals=0

time: 170 us -> 136 us (0.80)
  waiting for transfers between devices: 62.5 us -> 30.8 us
  blocking collectives: 43.1 us -> 32.4 us
  starting transfers between devices: 16.8 us -> 25.7 us
  Pallas kernels: 8.43 us -> 11.8 us
  local copies, waits for them, and re-layouts: 18.5 us -> 16.5 us
    all_gather x1 -> x0, blocking collectives: 22.3 us -> none  [local(): down = lax.all_gather(a_shared, 'dp', axis=0, tiled=True)]
    all_gather x1, waiting for transfers between devices: 24.4 us -> 8.48 us  [local(): lax.all_gather(by_y, 'mp', axis=0, tiled=True, axis_index_groups=along_z)]
    all_to_all x2 -> x4, waiting for transfers between devices: 38.2 us -> 22.3 us  [the longest x1 8.92 us: local(): lax.all_to_all(sent, 'mp', 0, 0, axis_index_groups=along_z)]
    all_to_all x0 -> x1, blocking collectives: none -> 11.7 us  [local(): lax.all_to_all(jnp.broadcast_to(scaled, (N_Z, 2 * own, rows)), 'mp', 0, 0...]
    all_to_all x2 -> x4, starting transfers between devices: 16.8 us -> 25.7 us  [the longest x1 9.95 us: local(): lax.all_to_all(sent, 'mp', 0, 0, axis_index_groups=along_z)]
    unnamed x18 -> x20, local copies, waits for them, and re-layouts: 5.15 us -> 0.06 us
    pallas_call x1, Pallas kernels: 8.43 us -> 11.8 us  [local(): pl.pallas_call(heads_kernel, grid=(N_Z,), in_specs=[pl.BlockSpec((block,...]
  transfers between devices with their start and end apart: 3 -> 5, of which waited for: 3 -> 4; matrix products, arithmetic and copies ran while one was open for 12% -> 15% of each run, Pallas kernels for 0% -> 0%
where the time goes in v2:
time: 136 us; the launch traced here: 135 us
  blocking collectives  32.4 us (24%)
  waiting for transfers between devices  30.8 us (23%)
  starting transfers between devices  25.7 us (19%)
  local copies, waits for them, and re-layouts  16.5 us (12%)
  between operations  13.6 us (10%)
  Pallas kernels  11.8 us (9%)
  other arithmetic  3.07 us (2%)
    all_gather x1, blocking collectives, local(): lax.all_gather(flat, 'mp', axis=0, tiled=True, axis_index_groups=along_y)  20.7 us
    pallas_call x1, Pallas kernels, local(): pl.pallas_call(heads_kernel, grid=(N_Z,), in_specs=[pl.BlockSpec((block,...  11.8 us
    all_to_all x1, blocking collectives, local(): lax.all_to_all(jnp.broadcast_to(scaled, (N_Z, 2 * own, rows)), 'mp', 0, 0...  11.7 us
    all_to_all x1, starting transfers between devices, local(): lax.all_to_all(sent, 'mp', 0, 0, axis_index_groups=along_z)  9.95 us
    all_to_all x1, waiting for transfers between devices, local(): lax.all_to_all(sent, 'mp', 0, 0, axis_index_groups=along_z)  8.92 us
    all_gather x1, waiting for transfers between devices, local(): lax.all_gather(by_y, 'mp', axis=0, tiled=True, axis_index_groups=along_z)  8.48 us
    all_to_all x1, starting transfers between devices, local(): lax.all_to_all(jnp.broadcast_to(a_shared, (groups, rank // groups, width)...  7.85 us
    all_to_all x1, waiting for transfers between devices, local(): down = lax.all_to_all(down, 'mp', 0, 0, axis_index_groups=along_y)  7.66 us
  transfers between devices with their start and end apart: 5, of which 4 were waited for; matrix products, arithmetic and copies ran while one was open for 15% of the time, Pallas kernels for 0%

profile of v2, /device:TPU:1, one launch (start us, length us, event | category | flops | bytes accessed | tf_op | source)
XLA Modules:
  0.0 135.0 jit_solution(17206502606498595512)
XLA Ops:
  6.5 20.7 %all_gather.6 = bf16[768,512]{1,0:T(8,128)(2,1)} all-gather(bf16[192,512]{1,0:T(8,128)(2,1)} %bitcast.51), channel_id=1, replica_groups={{0,8,16,24},{1,9,17,25},{2,10,18,26},{3,11,19,27},{4,12,20,28},{5,13,21..., dimensions={0}, use_global_device_ids=true | all-gather | bytes 983040 | tf_op jit(solution)/shard_map/all_gather | solution.py:79
  27.3 0.7 broadcast_in_dim.18
  28.0 7.9 %all-to-all-start = ((bf16[16,16,192]{2,1,0:T(8,128)(2,1)}), bf16[16,16,192]{2,1,0:T(8,128)(2,1)S(1)}, u32[]{:S(2)}, u32[]{:S(2)}) async-start(bf16[16,16,192]{2,1,0:T(8,128)(2,1)} %broadcast_in_dim.18), calls=%async_computation | async-start | bytes 262144 | tf_op jit(solution)/shard_map/all_to_all | solution.py:84
  35.8 0.2 convert_reduce_fusion
  36.1 0.3 fusion.3
  36.3 5.7 %all-to-all-done = bf16[16,16,192]{2,1,0:T(8,128)(2,1)S(1)} async-done(((bf16[16,16,192]{2,1,0:T(8,128)(2,1)}), bf16[16,16,192]{2,1,0:T(8,128)(2,1)S(1)}, u32[]{:S(2)}, u32[]{:S(2)}) %all-to-all-start) | async-done | bytes 98336 | tf_op jit(solution)/shard_map/all_to_all | solution.py:84
  42.1 0.8 maximum_maximum_fusion
  42.8 3.9 %all-to-all-start.1 = ((bf16[4,80,192]{2,1,0:T(8,128)(2,1)}), bf16[4,80,192]{2,1,0:T(8,128)(2,1)S(1)}, u32[]{:S(2)}, u32[]{:S(2)}) async-start(bf16[4,80,192]{2,1,0:T(8,128)(2,1)} %maximum_maximum_fusion), calls=%async_computation.1 | async-start | bytes 327680 | tf_op jit(solution)/shard_map/all_to_all | solution.py:93
  46.8 7.7 %all-to-all-done.1 = bf16[4,80,192]{2,1,0:T(8,128)(2,1)S(1)} async-done(((bf16[4,80,192]{2,1,0:T(8,128)(2,1)}), bf16[4,80,192]{2,1,0:T(8,128)(2,1)S(1)}, u32[]{:S(2)}, u32[]{:S(2)}) %all-to-all-start.1) | async-done | bytes 122912 | tf_op jit(solution)/shard_map/all_to_all | solution.py:93
  54.5 0.1 multiply_reduce_fusion
  54.9 0.1 copy.25
  55.1 0.1 reshape.238
  55.2 0.4 fusion.4
  55.6 0.7 pad_maximum_fusion
  56.3 10.0 %all-to-all-start.2 = ((bf16[8,16,512]{2,1,0:T(8,128)(2,1)}), bf16[8,16,512]{2,1,0:T(8,128)(2,1)S(1)}, u32[]{:S(2)}, u32[]{:S(2)}) async-start(bf16[8,16,512]{2,1,0:T(8,128)(2,1)} %pad_maximum_fusion), calls=%async_computation.2 | async-start | bytes 262144 | tf_op jit(solution)/shard_map/all_to_all | solution.py:123
  66.2 0.2 fusion.13
  66.4 0.2 fusion.15
  66.6 8.9 %all-to-all-done.2 = bf16[8,16,512]{2,1,0:T(8,128)(2,1)S(1)} async-done(((bf16[8,16,512]{2,1,0:T(8,128)(2,1)}), bf16[8,16,512]{2,1,0:T(8,128)(2,1)S(1)}, u32[]{:S(2)}, u32[]{:S(2)}) %all-to-all-start.2) | async-done | bytes 131104 | tf_op jit(solution)/shard_map/all_to_all | solution.py:123
  75.6 0.1 fusion.27
  76.1 11.7 %all_to_all.25 = bf16[8,16,512]{2,1,0:T(8,128)(2,1)S(1)} all-to-all(bf16[8,16,512]{2,1,0:T(8,128)(2,1)S(1)} %broadcast_in_dim.46), channel_id=1, replica_groups={{0,1,2,3,4,5,6,7},{8,9,10,11,12,13,14,15},{16,17,18,19,20,21,22,23},{24..., dimensions={0} | all-to-all | bytes 262144 | tf_op jit(solution)/shard_map/all_to_all | solution.py:145
  87.8 0.9 broadcast_in_dim.47
  88.6 4.0 %all-to-all-start.4 = ((bf16[4,8,16,512]{3,2,1,0:T(8,128)(2,1)}), bf16[4,8,16,512]{3,2,1,0:T(8,128)(2,1)S(1)}, u32[]{:S(2)}, u32[]{:S(2)}) async-start(bf16[4,8,16,512]{3,2,1,0:T(8,128)(2,1)} %broadcast_in_dim.47), calls=%async_computation.4 | async-start | bytes 1048576 | tf_op jit(solution)/shard_map/all_to_all | solution.py:148
  92.6 5.2 %copy.24 = bf16[8,384,4,192]{1,3,2,0:T(8,128)(2,1)} copy(bf16[8,384,4,192]{1,3,0,2:T(8,128)(2,1)} %bitcast.46) | data formatting | bytes 9437184 | tf_op jit(solution)/shard_map/transpose | solution.py:159
  97.8 6.7 %copy.28.w_ref = bf16[8,384,768]{2,1,0:T(8,128)(2,1)} copy(bf16[8,384,768]{1,2,0:T(8,128)(2,1)} %bitcast.45) | data formatting | bytes 9437184 | tf_op jit(solution)/shard_map/reshape | solution.py:159
  104.5 0.2 fusion.19
  104.7 0.2 fusion.20
  104.9 0.8 copy.27
  105.7 0.6 pad_maximum_fusion.2.stat_ref
  106.3 0.8 copy.26
  107.2 8.5 %all-gather.2.cloned.1.call-done.x_ref = bf16[6144,512]{1,0:T(8,128)(2,1)} async-done(((bf16[768,512]{1,0:T(8,128)(2,1)}), bf16[6144,512]{1,0:T(8,128)(2,1)}) %all-gather.2.cloned.1.call-update) | async-done | bytes 6291472 | tf_op jit(solution)/shard_map/all_gather | solution.py:80
  115.6 0.7 broadcast_in_dim.45.gain_ref
  116.3 11.8 %heads.1 = bf16[512,128]{1,0:T(8,128)(2,1)} custom-call(bf16[6144,512]{1,0:T(8,128)(2,1)} %all-gather.2.cloned.1.call-done.x_ref, bf16[8,384,768]{2,1,0:T(8,128)(2,1)} %copy.28.w_ref, f32[8,8,768]{2,1,0:T(8,128)} %broadcast_in_dim.45.gain_ref, f32[2,512]{1,0:T(2,128)} %pad_maximum_fusion.2.stat_ref, bf16[512,512]{1,0:T(8,128)(2,1)} %bitcast.47, ...), custom_call_target="tpu_custom_call" | custom-call | flops 2415919104 | bytes 12582912 | tf_op jit(solution)/shard_map/heads/pallas_call | solution.py:164
  (53 shorter events, 0.9 us)
Async XLA Ops:
  6.5 59.7 %copy-start = (f32[8,256]{1,0:T(8,128)S(1)}, f32[8,256]{1,0:T(8,128)}, u32[]{:S(2)}) copy-start(f32[8,256]{1,0:T(8,128)} %param.17) | copy-start | bytes 24580
  6.5 20.8 %copy-start.2 = (bf16[16,192]{1,0:T(8,128)(2,1)S(1)}, bf16[16,192]{1,0:T(8,128)(2,1)}, u32[]{:S(2)}) copy-start(bf16[16,192]{1,0:T(8,128)(2,1)} %param.14) | copy-start | bytes 18436
  6.5 109.1 %all-gather.2.cloned.1.call-start = ((), (), s32[]{:S(2)}) async-start(), calls=%async_computation.5 | async-start | bytes 7077888 | tf_op jit(solution)/shard_map/all_gather | solution.py:80
  27.3 8.6 %copy-start.1 = (bf16[768,512]{1,0:T(8,128)(2,1)S(1)}, bf16[768,512]{1,0:T(8,128)(2,1)}, u32[]{:S(2)}) copy-start(bf16[768,512]{1,0:T(8,128)(2,1)} %all_gather.6) | copy-start | bytes 2359300
  27.3 14.8 %copy-start.3 = (bf16[192]{0:T(256)(128)(2,1)S(1)}, bf16[192]{0:T(256)(128)(2,1)}, u32[]{:S(2)}) copy-start(bf16[192]{0:T(256)(128)(2,1)} %param.11) | copy-start | bytes 1156
  28.0 14.1 %all-to-all-start = ((bf16[16,16,192]{2,1,0:T(8,128)(2,1)}), bf16[16,16,192]{2,1,0:T(8,128)(2,1)S(1)}, u32[]{:S(2)}, u32[]{:S(2)}) async-start(bf16[16,16,192]{2,1,0:T(8,128)(2,1)} %broadcast_in_dim.18), calls=%async_computation | async-start | bytes 262144 | tf_op jit(solution)/shard_map/all_to_all | solution.py:84
  42.8 11.6 %all-to-all-start.1 = ((bf16[4,80,192]{2,1,0:T(8,128)(2,1)}), bf16[4,80,192]{2,1,0:T(8,128)(2,1)S(1)}, u32[]{:S(2)}, u32[]{:S(2)}) async-start(bf16[4,80,192]{2,1,0:T(8,128)(2,1)} %maximum_maximum_fusion), calls=%async_computation.1 | async-start | bytes 327680 | tf_op jit(solution)/shard_map/all_to_all | solution.py:93
  46.7 19.5 %copy-start.7 = (s32[2]{0:T(128)S(1)}, s32[2]{0:T(128)}, u32[]{:S(2)}) copy-start(s32[2]{0:T(128)} %param.12) | copy-start | bytes 28
  46.7 19.7 %copy-start.4 = (f32[8,256]{1,0:T(8,128)S(1)}, f32[8,256]{1,0:T(8,128)}, u32[]{:S(2)}) copy-start(f32[8,256]{1,0:T(8,128)} %param.16) | copy-start | bytes 24580
  56.3 19.3 %all-to-all-start.2 = ((bf16[8,16,512]{2,1,0:T(8,128)(2,1)}), bf16[8,16,512]{2,1,0:T(8,128)(2,1)S(1)}, u32[]{:S(2)}, u32[]{:S(2)}) async-start(bf16[8,16,512]{2,1,0:T(8,128)(2,1)} %pad_maximum_fusion), calls=%async_computation.2 | async-start | bytes 262144 | tf_op jit(solution)/shard_map/all_to_all | solution.py:123
  88.6 17.7 %all-to-all-start.4 = ((bf16[4,8,16,512]{3,2,1,0:T(8,128)(2,1)}), bf16[4,8,16,512]{3,2,1,0:T(8,128)(2,1)S(1)}, u32[]{:S(2)}, u32[]{:S(2)}) async-start(bf16[4,8,16,512]{3,2,1,0:T(8,128)(2,1)} %broadcast_in_dim.47), calls=%async_computation.4 | async-start | bytes 1048576 | tf_op jit(solution)/shard_map/all_to_all | solution.py:148
  97.8 6.7 %copy-start.5 = (f32[8,1,128]{2,1,0:T(1,128)S(1)}, f32[8,1,128]{2,1,0:T(1,128)}, u32[]{:S(2)}) copy-start(f32[8,1,128]{2,1,0:T(1,128)} %param.19) | copy-start | bytes 12292
  97.8 6.9 %copy-start.6 = (f32[8,1,128]{2,1,0:T(1,128)S(1)}, f32[8,1,128]{2,1,0:T(1,128)}, u32[]{:S(2)}) copy-start(f32[8,1,128]{2,1,0:T(1,128)} %param.18) | copy-start | bytes 12292
Sparse Core Ops, SparseCore 0:
  27.4 88.1 all-gather.1

commit v3 on v2

--- a/solution.py
+++ b/solution.py
@@ -24,23 +24,36 @@
     return (centre * lax.rsqrt(spread + eps)).astype(jnp.bfloat16)
 
 
-def heads_kernel(x_ref, w_ref, gain_ref, stat_ref, low_ref, b_ref, scale_ref, out_ref, acc_ref):
+def projected(x, w, gain, stat):
+    gain = jnp.transpose(jnp.broadcast_to(gain, (8, x.shape[0])))[:, :1]
+    normed = ((x.astype(jnp.float32) - stat[0:1]) * stat[1:2] * gain).astype(jnp.bfloat16)
+    return lax.dot_general(
+        w.reshape(x.shape[0], w.shape[-1]),
+        normed,
+        (((0,), (0,)), ((), ())),
+        preferred_element_type=jnp.float32,
+    )
+
+
+def heads_kernel(
+    x_ref, w_ref, gain_ref, stat_ref, low_ref, b_ref, scale_ref, out_ref, acc_ref
+):
     step = pl.program_id(0)
 
     @pl.when(step == 0)
     def _():
         acc_ref[...] = jnp.zeros_like(acc_ref)
 
-    gain = jnp.transpose(gain_ref[0])[:, :1]
-    centre = x_ref[...].astype(jnp.float32) - stat_ref[0:1, :]
-    normed = (centre * stat_ref[1:2, :] * gain).astype(jnp.bfloat16)
-    acc_ref[...] += jnp.dot(w_ref[0], normed, preferred_element_type=jnp.float32)
+    stat = stat_ref[...]
+    acc_ref[...] += sum(
+        projected(x_ref[n], w_ref[:, n], gain_ref[n], stat) for n in range(x_ref.shape[0])
+    )
 
     @pl.when(step == pl.num_programs(0) - 1)
     def _():
         size = b_ref.shape[0]
         images = scale_ref.shape[1] // 2
-        patches = x_ref.shape[1] // images
+        patches = x_ref.shape[2] // images
         rank = b_ref.shape[1]
         up_q = jnp.dot(b_ref[...], low_ref[:rank], preferred_element_type=jnp.float32)
         up_v = jnp.dot(b_ref[...], low_ref[rank:], preferred_element_type=jnp.float32)
@@ -155,19 +168,16 @@
     scale = jnp.concatenate((bq, bv), axis=0).T
     stat = jnp.stack((row_mean, row_scale), axis=0)
     outs = w_qkv.shape[2]
-    weights = (
-        w_qkv.reshape(N_Y, N_Z, width, outs).transpose(1, 3, 0, 2).reshape(N_Z, outs, block)
-    )
+    weights = w_qkv.reshape(N_Y, N_Z, width, outs)
     gains = gains.reshape(N_Z, 1, block)
-    gains = jnp.broadcast_to(gains, (N_Z, 8, block))
 
     result = pl.pallas_call(
         heads_kernel,
-        grid=(N_Z,),
+        grid=(N_Z // 2,),
         in_specs=[
-            pl.BlockSpec((block, rows), lambda i: (i, 0)),
-            pl.BlockSpec((1, outs, block), lambda i: (i, 0, 0)),
-            pl.BlockSpec((1, 8, block), lambda i: (i, 0, 0)),
+            pl.BlockSpec((2, block, rows), lambda i: (i, 0, 0)),
+            pl.BlockSpec((N_Y, 2, width, outs), lambda i: (0, i, 0, 0)),
+            pl.BlockSpec((2, 1, block), lambda i: (i, 0, 0)),
             pl.BlockSpec((2, rows), lambda i: (0, 0)),
             pl.BlockSpec((2 * rank, rows), lambda i: (0, 0)),
             pl.BlockSpec((size, rank), lambda i: (0, 0)),
@@ -183,7 +193,7 @@
             flops=2 * full * outs * rows, bytes_accessed=12 * 2**20, transcendentals=0
         ),
         name="heads",
-    )(whole, weights, gains, stat, low, b_shared.reshape(size, rank), scale)
+    )(whole.reshape(N_Z, block, rows), weights, gains, stat, low, b_shared.reshape(size, rank), scale)
     return result.reshape(rows, 1, size)
 
 

time: 136 us -> 132 us (0.971)
  local copies, waits for them, and re-layouts: 16.5 us -> 4.45 us
  waiting for transfers between devices: 30.8 us -> 42.2 us
  Pallas kernels: 11.8 us -> 9.38 us
    all_to_all x1, waiting for transfers between devices: 0.01 us -> 8.18 us  [local(): lax.all_to_all(jnp.broadcast_to(low, (N_Y, N_Z, 2 * own, rows)), 'mp', 0,...]
    reshape x1, local copies, waits for them, and re-layouts: 6.74 us -> 0.63 us  [local(): gains = gains.reshape(N_Z, 1, block)]
    transpose x1 -> x0, local copies, waits for them, and re-layouts: 5.16 us -> none  [local(): w_qkv.reshape(N_Y, N_Z, width, outs).transpose(1, 3, 0, 2)]
    all_gather x1, waiting for transfers between devices: 8.48 us -> 11.7 us  [local(): lax.all_gather(by_y, 'mp', axis=0, tiled=True, axis_index_groups=along_z)]
    pallas_call x1, Pallas kernels: 11.8 us -> 9.38 us  [local(): pl.pallas_call(heads_kernel, grid=(N_Z // 2,), in_specs=[pl.BlockSpec((2,...]
  transfers between devices with their start and end apart: 5 -> 5, of which waited for: 4 -> 5; matrix products, arithmetic and copies ran while one was open for 15% -> 7% of each run, Pallas kernels for 0% -> 0%
where the time goes in v3:
time: 132 us
  waiting for transfers between devices  42.2 us (32%)
  blocking collectives  32.5 us (25%)
  starting transfers between devices  25.6 us (19%)
  between operations  13.6 us (10%)
  Pallas kernels  9.38 us (7%)
  local copies, waits for them, and re-layouts  4.45 us (3%)
  other arithmetic  3.08 us (2%)
    all_gather x1, blocking collectives, local(): lax.all_gather(flat, 'mp', axis=0, tiled=True, axis_index_groups=along_y)  20.8 us
    all_to_all x1, blocking collectives, local(): lax.all_to_all(jnp.broadcast_to(scaled, (N_Z, 2 * own, rows)), 'mp', 0, 0...  11.7 us
    all_gather x1, waiting for transfers between devices, local(): lax.all_gather(by_y, 'mp', axis=0, tiled=True, axis_index_groups=along_z)  11.7 us
    all_to_all x1, starting transfers between devices, local(): lax.all_to_all(sent, 'mp', 0, 0, axis_index_groups=along_z)  9.96 us
    pallas_call x1, Pallas kernels, local(): pl.pallas_call(heads_kernel, grid=(N_Z // 2,), in_specs=[pl.BlockSpec((2,...  9.38 us
    all_to_all x1, waiting for transfers between devices, local(): lax.all_to_all(sent, 'mp', 0, 0, axis_index_groups=along_z)  8.93 us
    all_to_all x1, waiting for transfers between devices, local(): lax.all_to_all(jnp.broadcast_to(low, (N_Y, N_Z, 2 * own, rows)), 'mp', 0,...  8.18 us
    all_to_all x1, starting transfers between devices, local(): lax.all_to_all(jnp.broadcast_to(a_shared, (groups, rank // groups, width)...  7.78 us
  transfers between devices with their start and end apart: 5, of which 5 were waited for; matrix products, arithmetic and copies ran while one was open for 7% of the time, Pallas kernels for 0%

profile of v3, /device:TPU:1, one launch (start us, length us, event | category | flops | bytes accessed | tf_op | source)
XLA Modules:
  0.0 131.9 jit_solution(1101914915570129261)
XLA Ops:
  6.5 20.8 %all_gather.6 = bf16[768,512]{1,0:T(8,128)(2,1)} all-gather(bf16[192,512]{1,0:T(8,128)(2,1)} %bitcast.49), channel_id=1, replica_groups={{0,8,16,24},{1,9,17,25},{2,10,18,26},{3,11,19,27},{4,12,20,28},{5,13,21..., dimensions={0}, use_global_device_ids=true | all-gather | bytes 983040 | tf_op jit(solution)/shard_map/all_gather | solution.py:92
  27.4 0.7 broadcast_in_dim.16
  28.0 7.8 %all-to-all-start = ((bf16[16,16,192]{2,1,0:T(8,128)(2,1)}), bf16[16,16,192]{2,1,0:T(8,128)(2,1)S(1)}, u32[]{:S(2)}, u32[]{:S(2)}) async-start(bf16[16,16,192]{2,1,0:T(8,128)(2,1)} %broadcast_in_dim.16), calls=%async_computation | async-start | bytes 262144 | tf_op jit(solution)/shard_map/all_to_all | solution.py:97
  35.8 0.2 convert_reduce_fusion
  36.1 0.3 fusion.3
  36.3 5.7 %all-to-all-done = bf16[16,16,192]{2,1,0:T(8,128)(2,1)S(1)} async-done(((bf16[16,16,192]{2,1,0:T(8,128)(2,1)}), bf16[16,16,192]{2,1,0:T(8,128)(2,1)S(1)}, u32[]{:S(2)}, u32[]{:S(2)}) %all-to-all-start) | async-done | bytes 98336 | tf_op jit(solution)/shard_map/all_to_all | solution.py:97
  42.1 0.8 maximum_maximum_fusion
  42.8 3.9 %all-to-all-start.1 = ((bf16[4,80,192]{2,1,0:T(8,128)(2,1)}), bf16[4,80,192]{2,1,0:T(8,128)(2,1)S(1)}, u32[]{:S(2)}, u32[]{:S(2)}) async-start(bf16[4,80,192]{2,1,0:T(8,128)(2,1)} %maximum_maximum_fusion), calls=%async_computation.1 | async-start | bytes 327680 | tf_op jit(solution)/shard_map/all_to_all | solution.py:106
  46.8 7.7 %all-to-all-done.1 = bf16[4,80,192]{2,1,0:T(8,128)(2,1)S(1)} async-done(((bf16[4,80,192]{2,1,0:T(8,128)(2,1)}), bf16[4,80,192]{2,1,0:T(8,128)(2,1)S(1)}, u32[]{:S(2)}, u32[]{:S(2)}) %all-to-all-start.1) | async-done | bytes 122912 | tf_op jit(solution)/shard_map/all_to_all | solution.py:106
  54.5 0.1 reshape_squeeze.3
  54.6 0.1 copy.26
  54.7 0.1 reshape.239
  54.8 0.1 multiply_reduce_fusion
  55.2 0.3 fusion.4
  55.6 0.7 pad_maximum_fusion
  56.3 10.0 %all-to-all-start.2 = ((bf16[8,16,512]{2,1,0:T(8,128)(2,1)}), bf16[8,16,512]{2,1,0:T(8,128)(2,1)S(1)}, u32[]{:S(2)}, u32[]{:S(2)}) async-start(bf16[8,16,512]{2,1,0:T(8,128)(2,1)} %pad_maximum_fusion), calls=%async_computation.2 | async-start | bytes 262144 | tf_op jit(solution)/shard_map/all_to_all | solution.py:136
  66.2 0.2 fusion.15
  66.4 0.2 fusion.13
  66.6 8.9 %all-to-all-done.2 = bf16[8,16,512]{2,1,0:T(8,128)(2,1)S(1)} async-done(((bf16[8,16,512]{2,1,0:T(8,128)(2,1)}), bf16[8,16,512]{2,1,0:T(8,128)(2,1)S(1)}, u32[]{:S(2)}, u32[]{:S(2)}) %all-to-all-start.2) | async-done | bytes 131104 | tf_op jit(solution)/shard_map/all_to_all | solution.py:136
  75.6 0.1 fusion.27
  76.1 11.7 %all_to_all.25 = bf16[8,16,512]{2,1,0:T(8,128)(2,1)S(1)} all-to-all(bf16[8,16,512]{2,1,0:T(8,128)(2,1)S(1)} %broadcast_in_dim.40), channel_id=1, replica_groups={{0,1,2,3,4,5,6,7},{8,9,10,11,12,13,14,15},{16,17,18,19,20,21,22,23},{24..., dimensions={0} | all-to-all | bytes 262144 | tf_op jit(solution)/shard_map/all_to_all | solution.py:158
  87.8 0.8 broadcast_in_dim.41
  88.6 4.0 %all-to-all-start.4 = ((bf16[4,8,16,512]{3,2,1,0:T(8,128)(2,1)}), bf16[4,8,16,512]{3,2,1,0:T(8,128)(2,1)S(1)}, u32[]{:S(2)}, u32[]{:S(2)}) async-start(bf16[4,8,16,512]{3,2,1,0:T(8,128)(2,1)} %broadcast_in_dim.41), calls=%async_computation.4 | async-start | bytes 1048576 | tf_op jit(solution)/shard_map/all_to_all | solution.py:161
  92.6 0.2 fusion.20
  92.8 0.2 fusion.19
  93.0 0.7 copy.28
  93.7 0.6 reshape.244.gain_ref
  94.4 0.6 pad_maximum_fusion.2.stat_ref
  95.0 8.2 %all-to-all-done.4 = bf16[4,8,16,512]{3,2,1,0:T(8,128)(2,1)S(1)} async-done(((bf16[4,8,16,512]{3,2,1,0:T(8,128)(2,1)}), bf16[4,8,16,512]{3,2,1,0:T(8,128)(2,1)S(1)}, u32[]{:S(2)}, u32[]{:S(2)}) %all-to-all-start.4) | async-done | bytes 524320 | tf_op jit(solution)/shard_map/all_to_all | solution.py:161
  103.2 0.8 copy.27
  104.0 11.7 %all-gather.2.cloned.1.call-done = bf16[6144,512]{1,0:T(8,128)(2,1)} async-done(((bf16[768,512]{1,0:T(8,128)(2,1)}), bf16[6144,512]{1,0:T(8,128)(2,1)}) %all-gather.2.cloned.1.call-update) | async-done | bytes 6291472 | tf_op jit(solution)/shard_map/all_gather | solution.py:93
  115.6 9.4 %heads.1 = bf16[512,128]{1,0:T(8,128)(2,1)} custom-call(bf16[8,768,512]{2,1,0:T(8,128)(2,1)} %bitcast.43, bf16[4,8,192,384]{3,2,1,0:T(8,128)(2,1)} %bitcast.44, f32[8,1,768]{2,1,0:T(1,128)} %reshape.244.gain_ref, f32[2,512]{1,0:T(2,128)} %pad_maximum_fusion.2.stat_ref, bf16[512,512]{1,0:T(8,128)(2,1)} %bitcast.45, bf16[128,256]{1,0:T(8,128)(2,1)} %bitcast.52, ...), custom_call_target="tpu_custom_call" | custom-call | flops 2415919104 | bytes 12582912 | tf_op jit(solution)/shard_map/heads/pallas_call | solution.py:174
  (51 shorter events, 0.8 us)
Async XLA Ops:
  6.5 59.7 %copy-start = (f32[8,256]{1,0:T(8,128)S(1)}, f32[8,256]{1,0:T(8,128)}, u32[]{:S(2)}) copy-start(f32[8,256]{1,0:T(8,128)} %param.16) | copy-start | bytes 24580
  6.5 20.8 %copy-start.2 = (bf16[16,192]{1,0:T(8,128)(2,1)S(1)}, bf16[16,192]{1,0:T(8,128)(2,1)}, u32[]{:S(2)}) copy-start(bf16[16,192]{1,0:T(8,128)(2,1)} %param.14) | copy-start | bytes 18436
  6.5 109.1 %all-gather.2.cloned.1.call-start = ((), (), s32[]{:S(2)}) async-start(), calls=%async_computation.5 | async-start | bytes 7077888 | tf_op jit(solution)/shard_map/all_gather | solution.py:93
  27.3 8.5 %copy-start.1 = (bf16[768,512]{1,0:T(8,128)(2,1)S(1)}, bf16[768,512]{1,0:T(8,128)(2,1)}, u32[]{:S(2)}) copy-start(bf16[768,512]{1,0:T(8,128)(2,1)} %all_gather.6) | copy-start | bytes 2359300
  27.3 14.7 %copy-start.3 = (bf16[192]{0:T(256)(128)(2,1)S(1)}, bf16[192]{0:T(256)(128)(2,1)}, u32[]{:S(2)}) copy-start(bf16[192]{0:T(256)(128)(2,1)} %param.11) | copy-start | bytes 1156
  28.0 14.0 %all-to-all-start = ((bf16[16,16,192]{2,1,0:T(8,128)(2,1)}), bf16[16,16,192]{2,1,0:T(8,128)(2,1)S(1)}, u32[]{:S(2)}, u32[]{:S(2)}) async-start(bf16[16,16,192]{2,1,0:T(8,128)(2,1)} %broadcast_in_dim.16), calls=%async_computation | async-start | bytes 262144 | tf_op jit(solution)/shard_map/all_to_all | solution.py:97
  42.8 11.7 %all-to-all-start.1 = ((bf16[4,80,192]{2,1,0:T(8,128)(2,1)}), bf16[4,80,192]{2,1,0:T(8,128)(2,1)S(1)}, u32[]{:S(2)}, u32[]{:S(2)}) async-start(bf16[4,80,192]{2,1,0:T(8,128)(2,1)} %maximum_maximum_fusion), calls=%async_computation.1 | async-start | bytes 327680 | tf_op jit(solution)/shard_map/all_to_all | solution.py:106
  46.7 19.5 %copy-start.7 = (s32[2]{0:T(128)S(1)}, s32[2]{0:T(128)}, u32[]{:S(2)}) copy-start(s32[2]{0:T(128)} %param.12) | copy-start | bytes 28
  46.7 19.7 %copy-start.4 = (f32[8,256]{1,0:T(8,128)S(1)}, f32[8,256]{1,0:T(8,128)}, u32[]{:S(2)}) copy-start(f32[8,256]{1,0:T(8,128)} %param.17) | copy-start | bytes 24580
  56.3 19.3 %all-to-all-start.2 = ((bf16[8,16,512]{2,1,0:T(8,128)(2,1)}), bf16[8,16,512]{2,1,0:T(8,128)(2,1)S(1)}, u32[]{:S(2)}, u32[]{:S(2)}) async-start(bf16[8,16,512]{2,1,0:T(8,128)(2,1)} %pad_maximum_fusion), calls=%async_computation.2 | async-start | bytes 262144 | tf_op jit(solution)/shard_map/all_to_all | solution.py:136
  66.6 26.0 %copy-start.5 = (f32[8,1,128]{2,1,0:T(1,128)S(1)}, f32[8,1,128]{2,1,0:T(1,128)}, u32[]{:S(2)}) copy-start(f32[8,1,128]{2,1,0:T(1,128)} %param.18) | copy-start | bytes 12292
  66.6 26.2 %copy-start.6 = (f32[8,1,128]{2,1,0:T(1,128)S(1)}, f32[8,1,128]{2,1,0:T(1,128)}, u32[]{:S(2)}) copy-start(f32[8,1,128]{2,1,0:T(1,128)} %param.19) | copy-start | bytes 12292
  88.6 14.5 %all-to-all-start.4 = ((bf16[4,8,16,512]{3,2,1,0:T(8,128)(2,1)}), bf16[4,8,16,512]{3,2,1,0:T(8,128)(2,1)S(1)}, u32[]{:S(2)}, u32[]{:S(2)}) async-start(bf16[4,8,16,512]{3,2,1,0:T(8,128)(2,1)} %broadcast_in_dim.41), calls=%async_computation.4 | async-start | bytes 1048576 | tf_op jit(solution)/shard_map/all_to_all | solution.py:161
Sparse Core Ops, SparseCore 0:
  27.5 88.1 all-gather.1

commit v4 on v3

--- a/solution.py
+++ b/solution.py
@@ -173,11 +173,11 @@
 
     result = pl.pallas_call(
         heads_kernel,
-        grid=(N_Z // 2,),
+        grid=(N_Z // 4,),
         in_specs=[
-            pl.BlockSpec((2, block, rows), lambda i: (i, 0, 0)),
-            pl.BlockSpec((N_Y, 2, width, outs), lambda i: (0, i, 0, 0)),
-            pl.BlockSpec((2, 1, block), lambda i: (i, 0, 0)),
+            pl.BlockSpec((4, block, rows), lambda i: (i, 0, 0)),
+            pl.BlockSpec((N_Y, 4, width, outs), lambda i: (0, i, 0, 0)),
+            pl.BlockSpec((4, 1, block), lambda i: (i, 0, 0)),
             pl.BlockSpec((2, rows), lambda i: (0, 0)),
             pl.BlockSpec((2 * rank, rows), lambda i: (0, 0)),
             pl.BlockSpec((size, rank), lambda i: (0, 0)),
@@ -187,7 +187,7 @@
         out_shape=jax.ShapeDtypeStruct((rows, size), jnp.bfloat16),
         scratch_shapes=[pltpu.VMEM((outs, rows), jnp.float32)],
         compiler_params=pltpu.CompilerParams(
-            dimension_semantics=("arbitrary",), vmem_limit_bytes=56 * 2**20
+            dimension_semantics=("arbitrary",), vmem_limit_bytes=52 * 2**20
         ),
         cost_estimate=pl.CostEstimate(
             flops=2 * full * outs * rows, bytes_accessed=12 * 2**20, transcendentals=0

time: 132 us -> 132 us (level)
  waiting for transfers between devices: 42.2 us -> 44.7 us
  local copies, waits for them, and re-layouts: 4.45 us -> 2.42 us
    all_to_all x1, waiting for transfers between devices: 8.18 us -> 10 us  [local(): lax.all_to_all(jnp.broadcast_to(low, (N_Y, N_Z, 2 * own, rows)), 'mp', 0,...]
  transfers between devices with their start and end apart: 5 -> 5, of which waited for: 5 -> 5; matrix products, arithmetic and copies ran while one was open for 7% -> 5% of each run, Pallas kernels for 0% -> 0%
where the time goes in v4:
time: 132 us; the launch traced here: 131 us
  waiting for transfers between devices  44.7 us (34%)
  blocking collectives  32.4 us (25%)
  starting transfers between devices  25.8 us (20%)
  between operations  13.6 us (10%)
  Pallas kernels  8.52 us (6%)
  other arithmetic  2.49 us (2%)
  local copies, waits for them, and re-layouts  2.42 us (2%)
    all_gather x1, blocking collectives, local(): lax.all_gather(flat, 'mp', axis=0, tiled=True, axis_index_groups=along_y)  20.7 us
    all_gather x1, waiting for transfers between devices, local(): lax.all_gather(by_y, 'mp', axis=0, tiled=True, axis_index_groups=along_z)  12.4 us
    all_to_all x1, blocking collectives, local(): lax.all_to_all(jnp.broadcast_to(scaled, (N_Z, 2 * own, rows)), 'mp', 0, 0...  11.7 us
    all_to_all x1, waiting for transfers between devices, local(): lax.all_to_all(jnp.broadcast_to(low, (N_Y, N_Z, 2 * own, rows)), 'mp', 0,...  10 us
    all_to_all x1, starting transfers between devices, local(): lax.all_to_all(sent, 'mp', 0, 0, axis_index_groups=along_z)  9.99 us
    all_to_all x1, waiting for transfers between devices, local(): lax.all_to_all(sent, 'mp', 0, 0, axis_index_groups=along_z)  8.93 us
    pallas_call x1, Pallas kernels, local(): pl.pallas_call(heads_kernel, grid=(N_Z // 4,), in_specs=[pl.BlockSpec((4,...  8.52 us
    all_to_all x1, starting transfers between devices, local(): lax.all_to_all(jnp.broadcast_to(a_shared, (groups, rank // groups, width)...  7.87 us
  transfers between devices with their start and end apart: 5, of which 5 were waited for; matrix products, arithmetic and copies ran while one was open for 5% of the time, Pallas kernels for 0%

profile of v4, /device:TPU:1, one launch (start us, length us, event | category | flops | bytes accessed | tf_op | source)
XLA Modules:
  0.0 131.0 jit_solution(12542748877187073805)
XLA Ops:
  6.5 20.7 %all_gather.6 = bf16[768,512]{1,0:T(8,128)(2,1)} all-gather(bf16[192,512]{1,0:T(8,128)(2,1)} %bitcast.50), channel_id=1, replica_groups={{0,8,16,24},{1,9,17,25},{2,10,18,26},{3,11,19,27},{4,12,20,28},{5,13,21..., dimensions={0}, use_global_device_ids=true | all-gather | bytes 983040 | tf_op jit(solution)/shard_map/all_gather | solution.py:92
  27.3 0.7 broadcast_in_dim.16
  28.0 7.9 %all-to-all-start = ((bf16[16,16,192]{2,1,0:T(8,128)(2,1)}), bf16[16,16,192]{2,1,0:T(8,128)(2,1)S(1)}, u32[]{:S(2)}, u32[]{:S(2)}) async-start(bf16[16,16,192]{2,1,0:T(8,128)(2,1)} %broadcast_in_dim.16), calls=%async_computation | async-start | bytes 262144 | tf_op jit(solution)/shard_map/all_to_all | solution.py:97
  35.8 0.2 convert_reduce_fusion
  36.1 0.3 fusion.3
  36.3 5.7 %all-to-all-done = bf16[16,16,192]{2,1,0:T(8,128)(2,1)S(1)} async-done(((bf16[16,16,192]{2,1,0:T(8,128)(2,1)}), bf16[16,16,192]{2,1,0:T(8,128)(2,1)S(1)}, u32[]{:S(2)}, u32[]{:S(2)}) %all-to-all-start) | async-done | bytes 98336 | tf_op jit(solution)/shard_map/all_to_all | solution.py:97
  42.1 0.8 maximum_maximum_fusion
  42.8 3.9 %all-to-all-start.1 = ((bf16[4,80,192]{2,1,0:T(8,128)(2,1)}), bf16[4,80,192]{2,1,0:T(8,128)(2,1)S(1)}, u32[]{:S(2)}, u32[]{:S(2)}) async-start(bf16[4,80,192]{2,1,0:T(8,128)(2,1)} %maximum_maximum_fusion), calls=%async_computation.1 | async-start | bytes 327680 | tf_op jit(solution)/shard_map/all_to_all | solution.py:106
  46.8 7.7 %all-to-all-done.1 = bf16[4,80,192]{2,1,0:T(8,128)(2,1)S(1)} async-done(((bf16[4,80,192]{2,1,0:T(8,128)(2,1)}), bf16[4,80,192]{2,1,0:T(8,128)(2,1)S(1)}, u32[]{:S(2)}, u32[]{:S(2)}) %all-to-all-start.1) | async-done | bytes 122912 | tf_op jit(solution)/shard_map/all_to_all | solution.py:106
  54.5 0.1 reshape_squeeze.3
  54.6 0.1 copy.26
  54.7 0.1 reshape.239
  54.8 0.1 multiply_reduce_fusion
  55.0 0.1 reshape.241
  55.1 0.1 concatenate.13
  55.2 0.3 fusion.4
  55.5 0.7 pad_maximum_fusion
  56.2 10.0 %all-to-all-start.2 = ((bf16[8,16,512]{2,1,0:T(8,128)(2,1)}), bf16[8,16,512]{2,1,0:T(8,128)(2,1)S(1)}, u32[]{:S(2)}, u32[]{:S(2)}) async-start(bf16[8,16,512]{2,1,0:T(8,128)(2,1)} %pad_maximum_fusion), calls=%async_computation.2 | async-start | bytes 262144 | tf_op jit(solution)/shard_map/all_to_all | solution.py:136
  66.2 0.2 fusion.15
  66.4 0.2 fusion.13
  66.6 8.9 %all-to-all-done.2 = bf16[8,16,512]{2,1,0:T(8,128)(2,1)S(1)} async-done(((bf16[8,16,512]{2,1,0:T(8,128)(2,1)}), bf16[8,16,512]{2,1,0:T(8,128)(2,1)S(1)}, u32[]{:S(2)}, u32[]{:S(2)}) %all-to-all-start.2) | async-done | bytes 131104 | tf_op jit(solution)/shard_map/all_to_all | solution.py:136
  75.6 0.1 fusion.27
  75.9 0.1 fusion.8
  76.1 11.7 %all_to_all.25 = bf16[8,16,512]{2,1,0:T(8,128)(2,1)S(1)} all-to-all(bf16[8,16,512]{2,1,0:T(8,128)(2,1)S(1)} %broadcast_in_dim.40), channel_id=1, replica_groups={{0,1,2,3,4,5,6,7},{8,9,10,11,12,13,14,15},{16,17,18,19,20,21,22,23},{24..., dimensions={0} | all-to-all | bytes 262144 | tf_op jit(solution)/shard_map/all_to_all | solution.py:158
  87.8 0.8 broadcast_in_dim.41
  88.6 4.0 %all-to-all-start.4 = ((bf16[4,8,16,512]{3,2,1,0:T(8,128)(2,1)}), bf16[4,8,16,512]{3,2,1,0:T(8,128)(2,1)S(1)}, u32[]{:S(2)}, u32[]{:S(2)}) async-start(bf16[4,8,16,512]{3,2,1,0:T(8,128)(2,1)} %broadcast_in_dim.41), calls=%async_computation.4 | async-start | bytes 1048576 | tf_op jit(solution)/shard_map/all_to_all | solution.py:161
  92.6 0.2 fusion.20
  92.8 0.2 fusion.19
  93.0 0.1 copy.28
  93.2 10.0 %all-to-all-done.4 = bf16[4,8,16,512]{3,2,1,0:T(8,128)(2,1)S(1)} async-done(((bf16[4,8,16,512]{3,2,1,0:T(8,128)(2,1)}), bf16[4,8,16,512]{3,2,1,0:T(8,128)(2,1)S(1)}, u32[]{:S(2)}, u32[]{:S(2)}) %all-to-all-start.4) | async-done | bytes 524320 | tf_op jit(solution)/shard_map/all_to_all | solution.py:161
  103.2 12.4 %all-gather.2.cloned.1.call-done = bf16[6144,512]{1,0:T(8,128)(2,1)} async-done(((bf16[768,512]{1,0:T(8,128)(2,1)}), bf16[6144,512]{1,0:T(8,128)(2,1)}) %all-gather.2.cloned.1.call-update) | async-done | bytes 6291472 | tf_op jit(solution)/shard_map/all_gather | solution.py:93
  115.7 8.5 %heads.1 = bf16[512,128]{1,0:T(8,128)(2,1)} custom-call(bf16[8,768,512]{2,1,0:T(8,128)(2,1)} %bitcast.46, bf16[4,8,192,384]{3,2,1,0:T(8,128)(2,1)} %bitcast.47, f32[8,1,768]{2,1,0:T(1,128)S(1)} %reshape.244.gain_ref, f32[2,512]{1,0:T(2,128)S(1)} %pad_maximum_fusion.2.stat_ref, bf16[512,512]{1,0:T(8,128)(2,1)S(1)} %bitcast.43, bf16[128,256]{1,0:T(8,128)(2,1)S(1)} %bitcast.45, ...), custom_call_target="tpu_custom_call" | custom-call | flops 2415919104 | bytes 12582912 | tf_op jit(solution)/shard_map/heads/pallas_call | solution.py:174
  (53 shorter events, 0.6 us)
Async XLA Ops:
  6.5 59.7 %copy-start = (f32[8,256]{1,0:T(8,128)S(1)}, f32[8,256]{1,0:T(8,128)}, u32[]{:S(2)}) copy-start(f32[8,256]{1,0:T(8,128)} %param.16) | copy-start | bytes 24580
  6.5 20.7 %copy-start.3 = (bf16[16,192]{1,0:T(8,128)(2,1)S(1)}, bf16[16,192]{1,0:T(8,128)(2,1)}, u32[]{:S(2)}) copy-start(bf16[16,192]{1,0:T(8,128)(2,1)} %param.14) | copy-start | bytes 18436
  6.5 109.1 %all-gather.2.cloned.1.call-start = ((), (), s32[]{:S(2)}) async-start(), calls=%async_computation.5 | async-start | bytes 7077888 | tf_op jit(solution)/shard_map/all_gather | solution.py:93
  27.3 8.6 %copy-start.2 = (bf16[768,512]{1,0:T(8,128)(2,1)S(1)}, bf16[768,512]{1,0:T(8,128)(2,1)}, u32[]{:S(2)}) copy-start(bf16[768,512]{1,0:T(8,128)(2,1)} %all_gather.6) | copy-start | bytes 2359300
  27.3 14.8 %copy-start.4 = (bf16[192]{0:T(256)(128)(2,1)S(1)}, bf16[192]{0:T(256)(128)(2,1)}, u32[]{:S(2)}) copy-start(bf16[192]{0:T(256)(128)(2,1)} %param.11) | copy-start | bytes 1156
  28.0 14.1 %all-to-all-start = ((bf16[16,16,192]{2,1,0:T(8,128)(2,1)}), bf16[16,16,192]{2,1,0:T(8,128)(2,1)S(1)}, u32[]{:S(2)}, u32[]{:S(2)}) async-start(bf16[16,16,192]{2,1,0:T(8,128)(2,1)} %broadcast_in_dim.16), calls=%async_computation | async-start | bytes 262144 | tf_op jit(solution)/shard_map/all_to_all | solution.py:97
  42.8 11.6 %all-to-all-start.1 = ((bf16[4,80,192]{2,1,0:T(8,128)(2,1)}), bf16[4,80,192]{2,1,0:T(8,128)(2,1)S(1)}, u32[]{:S(2)}, u32[]{:S(2)}) async-start(bf16[4,80,192]{2,1,0:T(8,128)(2,1)} %maximum_maximum_fusion), calls=%async_computation.1 | async-start | bytes 327680 | tf_op jit(solution)/shard_map/all_to_all | solution.py:106
  46.7 19.5 %copy-start.8 = (s32[2]{0:T(128)S(1)}, s32[2]{0:T(128)}, u32[]{:S(2)}) copy-start(s32[2]{0:T(128)} %param.12) | copy-start | bytes 28
  46.7 19.7 %copy-start.5 = (f32[8,256]{1,0:T(8,128)S(1)}, f32[8,256]{1,0:T(8,128)}, u32[]{:S(2)}) copy-start(f32[8,256]{1,0:T(8,128)} %param.17) | copy-start | bytes 24580
  56.2 19.3 %all-to-all-start.2 = ((bf16[8,16,512]{2,1,0:T(8,128)(2,1)}), bf16[8,16,512]{2,1,0:T(8,128)(2,1)S(1)}, u32[]{:S(2)}, u32[]{:S(2)}) async-start(bf16[8,16,512]{2,1,0:T(8,128)(2,1)} %pad_maximum_fusion), calls=%async_computation.2 | async-start | bytes 262144 | tf_op jit(solution)/shard_map/all_to_all | solution.py:136
  66.6 26.0 %copy-start.6 = (f32[8,1,128]{2,1,0:T(1,128)S(1)}, f32[8,1,128]{2,1,0:T(1,128)}, u32[]{:S(2)}) copy-start(f32[8,1,128]{2,1,0:T(1,128)} %param.18) | copy-start | bytes 12292
  66.6 26.2 %copy-start.7 = (f32[8,1,128]{2,1,0:T(1,128)S(1)}, f32[8,1,128]{2,1,0:T(1,128)}, u32[]{:S(2)}) copy-start(f32[8,1,128]{2,1,0:T(1,128)} %param.19) | copy-start | bytes 12292
  87.8 27.9 %copy-start.1 = (bf16[1,128,256]{2,1,0:T(8,128)(2,1)S(1)}, bf16[1,128,256]{2,1,0:T(8,128)(2,1)}, u32[]{:S(2)}) copy-start(bf16[1,128,256]{2,1,0:T(8,128)(2,1)} %param.15) | copy-start | bytes 196612
  88.6 14.6 %all-to-all-start.4 = ((bf16[4,8,16,512]{3,2,1,0:T(8,128)(2,1)}), bf16[4,8,16,512]{3,2,1,0:T(8,128)(2,1)S(1)}, u32[]{:S(2)}, u32[]{:S(2)}) async-start(bf16[4,8,16,512]{3,2,1,0:T(8,128)(2,1)} %broadcast_in_dim.41), calls=%async_computation.4 | async-start | bytes 1048576 | tf_op jit(solution)/shard_map/all_to_all | solution.py:161
Sparse Core Ops, SparseCore 0:
  27.4 88.2 all-gather.1

commit v5 on v4

--- a/solution.py
+++ b/solution.py
@@ -7,6 +7,7 @@
 
 eps = 1e-06
 N_Y, N_Z = 4, 8
+PATCHES = 256
 along_y = [[y * N_Z + z for y in range(N_Y)] for z in range(N_Z)]
 along_z = [[y * N_Z + z for z in range(N_Z)] for y in range(N_Y)]
 
@@ -36,7 +37,7 @@
 
 
 def heads_kernel(
-    x_ref, w_ref, gain_ref, stat_ref, low_ref, b_ref, scale_ref, out_ref, acc_ref
+    x_ref, w_ref, gain_ref, stat_ref, lift_ref, out_ref, acc_ref
 ):
     step = pl.program_id(0)
 
@@ -51,18 +52,12 @@
 
     @pl.when(step == pl.num_programs(0) - 1)
     def _():
-        size = b_ref.shape[0]
-        images = scale_ref.shape[1] // 2
-        patches = x_ref.shape[2] // images
-        rank = b_ref.shape[1]
-        up_q = jnp.dot(b_ref[...], low_ref[:rank], preferred_element_type=jnp.float32)
-        up_v = jnp.dot(b_ref[...], low_ref[rank:], preferred_element_type=jnp.float32)
-        for i in range(images):
+        size = out_ref.shape[1]
+        patches = PATCHES
+        for i in range(out_ref.shape[0] // patches):
             cols = slice(i * patches, (i + 1) * patches)
-            query = acc_ref[:size, cols] + up_q[:, cols] * scale_ref[:, i : i + 1]
-            value = (
-                acc_ref[2 * size :, cols] + up_v[:, cols] * scale_ref[:, images + i : images + i + 1]
-            ).astype(jnp.bfloat16)
+            query = acc_ref[:size, cols] + lift_ref[:size, cols]
+            value = (acc_ref[2 * size :, cols] + lift_ref[size:, cols]).astype(jnp.bfloat16)
             query = unit_columns(query)
             key = unit_columns(acc_ref[size : 2 * size, cols])
             scores = lax.dot_general(
@@ -165,7 +160,16 @@
 
     bq = jnp.dot(onehot, b_query.reshape(tasks, size), precision=highest)
     bv = jnp.dot(onehot, b_value.reshape(tasks, size), precision=highest)
-    scale = jnp.concatenate((bq, bv), axis=0).T
+    up = b_shared.reshape(size, rank)
+    lift = jnp.concatenate(
+        (
+            jnp.dot(up, low[:rank], preferred_element_type=jnp.float32)
+            * jnp.repeat(bq.T, patches, axis=1),
+            jnp.dot(up, low[rank:], preferred_element_type=jnp.float32)
+            * jnp.repeat(bv.T, patches, axis=1),
+        ),
+        axis=0,
+    )
     stat = jnp.stack((row_mean, row_scale), axis=0)
     outs = w_qkv.shape[2]
     weights = w_qkv.reshape(N_Y, N_Z, width, outs)
@@ -179,9 +183,7 @@
             pl.BlockSpec((N_Y, 4, width, outs), lambda i: (0, i, 0, 0)),
             pl.BlockSpec((4, 1, block), lambda i: (i, 0, 0)),
             pl.BlockSpec((2, rows), lambda i: (0, 0)),
-            pl.BlockSpec((2 * rank, rows), lambda i: (0, 0)),
-            pl.BlockSpec((size, rank), lambda i: (0, 0)),
-            pl.BlockSpec((size, 2 * images), lambda i: (0, 0)),
+            pl.BlockSpec((2 * size, rows), lambda i: (0, 0)),
         ],
         out_specs=pl.BlockSpec((rows, size), lambda i: (0, 0)),
         out_shape=jax.ShapeDtypeStruct((rows, size), jnp.bfloat16),
@@ -193,7 +195,7 @@
             flops=2 * full * outs * rows, bytes_accessed=12 * 2**20, transcendentals=0
         ),
         name="heads",
-    )(whole.reshape(N_Z, block, rows), weights, gains, stat, low, b_shared.reshape(size, rank), scale)
+    )(whole.reshape(N_Z, block, rows), weights, gains, stat, lift)
     return result.reshape(rows, 1, size)
 
 

time: 132 us -> 131 us (level)
  no operation moved by 1% of the time
where the time goes in v5:
time: 131 us
  waiting for transfers between devices  43.7 us (33%)
  blocking collectives  32.4 us (25%)
  starting transfers between devices  25.7 us (20%)
  between operations  13.7 us (10%)
  Pallas kernels  8.41 us (6%)
  local copies, waits for them, and re-layouts  2.95 us (2%)
  other arithmetic  2.51 us (2%)
  matrix products  1.48 us (1%)
    all_gather x1, blocking collectives, local(): lax.all_gather(flat, 'mp', axis=0, tiled=True, axis_index_groups=along_y)  20.7 us
    all_gather x1, waiting for transfers between devices, local(): lax.all_gather(by_y, 'mp', axis=0, tiled=True, axis_index_groups=along_z)  12 us
    all_to_all x1, blocking collectives, local(): lax.all_to_all(jnp.broadcast_to(scaled, (N_Z, 2 * own, rows)), 'mp', 0, 0...  11.7 us
    all_to_all x1, starting transfers between devices, local(): lax.all_to_all(sent, 'mp', 0, 0, axis_index_groups=along_z)  9.99 us
    all_to_all x1, waiting for transfers between devices, local(): lax.all_to_all(jnp.broadcast_to(low, (N_Y, N_Z, 2 * own, rows)), 'mp', 0,...  9.4 us
    all_to_all x1, waiting for transfers between devices, local(): lax.all_to_all(sent, 'mp', 0, 0, axis_index_groups=along_z)  8.93 us
    pallas_call x1, Pallas kernels, local(): pl.pallas_call(heads_kernel, grid=(N_Z // 4,), in_specs=[pl.BlockSpec((4,...  8.41 us
    all_to_all x1, starting transfers between devices, local(): lax.all_to_all(jnp.broadcast_to(a_shared, (groups, rank // groups, width)...  7.87 us
  transfers between devices with their start and end apart: 5, of which 5 were waited for; matrix products, arithmetic and copies ran while one was open for 5% of the time, Pallas kernels for 0%

profile of v5, /device:TPU:1, one launch (start us, length us, event | category | flops | bytes accessed | tf_op | source)
XLA Modules:
  0.0 130.9 jit_solution(14075290850018948915)
XLA Ops:
  6.5 20.7 %all_gather.6 = bf16[768,512]{1,0:T(8,128)(2,1)} all-gather(bf16[192,512]{1,0:T(8,128)(2,1)} %bitcast.76), channel_id=1, replica_groups={{0,8,16,24},{1,9,17,25},{2,10,18,26},{3,11,19,27},{4,12,20,28},{5,13,21..., dimensions={0}, use_global_device_ids=true | all-gather | bytes 983040 | tf_op jit(solution)/shard_map/all_gather | solution.py:87
  27.3 0.7 broadcast_in_dim.40
  28.0 7.9 %all-to-all-start = ((bf16[16,16,192]{2,1,0:T(8,128)(2,1)}), bf16[16,16,192]{2,1,0:T(8,128)(2,1)S(1)}, u32[]{:S(2)}, u32[]{:S(2)}) async-start(bf16[16,16,192]{2,1,0:T(8,128)(2,1)} %broadcast_in_dim.40), calls=%async_computation | async-start | bytes 262144 | tf_op jit(solution)/shard_map/all_to_all | solution.py:92
  35.8 0.2 convert_reduce_fusion
  36.1 0.3 fusion.3
  36.3 5.7 %all-to-all-done = bf16[16,16,192]{2,1,0:T(8,128)(2,1)S(1)} async-done(((bf16[16,16,192]{2,1,0:T(8,128)(2,1)}), bf16[16,16,192]{2,1,0:T(8,128)(2,1)S(1)}, u32[]{:S(2)}, u32[]{:S(2)}) %all-to-all-start) | async-done | bytes 98336 | tf_op jit(solution)/shard_map/all_to_all | solution.py:92
  42.1 0.8 maximum_maximum_fusion
  42.8 3.9 %all-to-all-start.1 = ((bf16[4,80,192]{2,1,0:T(8,128)(2,1)}), bf16[4,80,192]{2,1,0:T(8,128)(2,1)S(1)}, u32[]{:S(2)}, u32[]{:S(2)}) async-start(bf16[4,80,192]{2,1,0:T(8,128)(2,1)} %maximum_maximum_fusion), calls=%async_computation.1 | async-start | bytes 327680 | tf_op jit(solution)/shard_map/all_to_all | solution.py:101
  46.8 7.6 %all-to-all-done.1 = bf16[4,80,192]{2,1,0:T(8,128)(2,1)S(1)} async-done(((bf16[4,80,192]{2,1,0:T(8,128)(2,1)}), bf16[4,80,192]{2,1,0:T(8,128)(2,1)S(1)}, u32[]{:S(2)}, u32[]{:S(2)}) %all-to-all-start.1) | async-done | bytes 122912 | tf_op jit(solution)/shard_map/all_to_all | solution.py:101
  54.5 0.1 multiply_reduce_fusion
  54.9 0.1 copy.24
  55.1 0.1 reshape.245
  55.2 0.3 fusion.6
  55.6 0.7 pad_maximum_fusion.1
  56.2 10.0 %all-to-all-start.2 = ((bf16[8,16,512]{2,1,0:T(8,128)(2,1)}), bf16[8,16,512]{2,1,0:T(8,128)(2,1)S(1)}, u32[]{:S(2)}, u32[]{:S(2)}) async-start(bf16[8,16,512]{2,1,0:T(8,128)(2,1)} %pad_maximum_fusion.1), calls=%async_computation.2 | async-start | bytes 262144 | tf_op jit(solution)/shard_map/all_to_all | solution.py:131
  66.2 0.2 fusion.17
  66.4 0.2 fusion.19
  66.6 8.9 %all-to-all-done.2 = bf16[8,16,512]{2,1,0:T(8,128)(2,1)S(1)} async-done(((bf16[8,16,512]{2,1,0:T(8,128)(2,1)}), bf16[8,16,512]{2,1,0:T(8,128)(2,1)S(1)}, u32[]{:S(2)}, u32[]{:S(2)}) %all-to-all-start.2) | async-done | bytes 131104 | tf_op jit(solution)/shard_map/all_to_all | solution.py:131
  76.1 11.7 %all_to_all.25 = bf16[8,16,512]{2,1,0:T(8,128)(2,1)S(1)} all-to-all(bf16[8,16,512]{2,1,0:T(8,128)(2,1)S(1)} %broadcast_in_dim.46), channel_id=1, replica_groups={{0,1,2,3,4,5,6,7},{8,9,10,11,12,13,14,15},{16,17,18,19,20,21,22,23},{24..., dimensions={0} | all-to-all | bytes 262144 | tf_op jit(solution)/shard_map/all_to_all | solution.py:153
  87.8 0.8 broadcast_in_dim.47
  88.6 4.0 %all-to-all-start.4 = ((bf16[4,8,16,512]{3,2,1,0:T(8,128)(2,1)}), bf16[4,8,16,512]{3,2,1,0:T(8,128)(2,1)S(1)}, u32[]{:S(2)}, u32[]{:S(2)}) async-start(bf16[4,8,16,512]{3,2,1,0:T(8,128)(2,1)} %broadcast_in_dim.47), calls=%async_computation.4 | async-start | bytes 1048576 | tf_op jit(solution)/shard_map/all_to_all | solution.py:156
  92.6 0.2 convolution_bitcast_fusion.3
  92.8 0.1 copy.25
  92.9 0.2 broadcast_in_dim.48
  93.2 0.2 convolution_bitcast_fusion.2
  93.4 0.1 copy.26
  93.5 0.2 broadcast_in_dim.49
  93.8 9.4 %all-to-all-done.4 = bf16[4,8,16,512]{3,2,1,0:T(8,128)(2,1)S(1)} async-done(((bf16[4,8,16,512]{3,2,1,0:T(8,128)(2,1)}), bf16[4,8,16,512]{3,2,1,0:T(8,128)(2,1)S(1)}, u32[]{:S(2)}, u32[]{:S(2)}) %all-to-all-start.4) | async-done | bytes 524320 | tf_op jit(solution)/shard_map/all_to_all | solution.py:156
  103.2 0.2 fusion.5
  103.4 0.2 fusion.4
  103.6 12.0 %all-gather.2.cloned.1.call-done = bf16[6144,512]{1,0:T(8,128)(2,1)} async-done(((bf16[768,512]{1,0:T(8,128)(2,1)}), bf16[6144,512]{1,0:T(8,128)(2,1)}) %all-gather.2.cloned.1.call-update) | async-done | bytes 6291472 | tf_op jit(solution)/shard_map/all_gather | solution.py:88
  115.7 8.4 %heads.1 = bf16[512,128]{1,0:T(8,128)(2,1)} custom-call(bf16[8,768,512]{2,1,0:T(8,128)(2,1)} %bitcast.67, bf16[4,8,192,384]{3,2,1,0:T(8,128)(2,1)} %bitcast.68, f32[8,1,768]{2,1,0:T(1,128)S(1)} %reshape.250.gain_ref, f32[2,512]{1,0:T(2,128)S(1)} %pad_maximum_fusion.3.stat_ref, f32[256,512]{1,0:T(8,128)S(1)} %pad_maximum_fusion.lift_ref), custom_call_target="tpu_custom_call" | custom-call | flops 2415919104 | bytes 12582912 | tf_op jit(solution)/shard_map/heads/pallas_call | solution.py:178
  (59 shorter events, 1.1 us)
Async XLA Ops:
  6.5 96.6 %copy-start = (bf16[1,128,256]{2,1,0:T(8,128)(2,1)S(1)}, bf16[1,128,256]{2,1,0:T(8,128)(2,1)}, u32[]{:S(2)}) copy-start(bf16[1,128,256]{2,1,0:T(8,128)(2,1)} %param.15) | copy-start | bytes 196612
  6.5 20.7 %copy-start.2 = (bf16[16,192]{1,0:T(8,128)(2,1)S(1)}, bf16[16,192]{1,0:T(8,128)(2,1)}, u32[]{:S(2)}) copy-start(bf16[16,192]{1,0:T(8,128)(2,1)} %param.14) | copy-start | bytes 18436
  6.5 109.1 %all-gather.2.cloned.1.call-start = ((), (), s32[]{:S(2)}) async-start(), calls=%async_computation.5 | async-start | bytes 7077888 | tf_op jit(solution)/shard_map/all_gather | solution.py:88
  27.3 8.6 %copy-start.1 = (bf16[768,512]{1,0:T(8,128)(2,1)S(1)}, bf16[768,512]{1,0:T(8,128)(2,1)}, u32[]{:S(2)}) copy-start(bf16[768,512]{1,0:T(8,128)(2,1)} %all_gather.6) | copy-start | bytes 2359300
  27.3 14.8 %copy-start.3 = (bf16[192]{0:T(256)(128)(2,1)S(1)}, bf16[192]{0:T(256)(128)(2,1)}, u32[]{:S(2)}) copy-start(bf16[192]{0:T(256)(128)(2,1)} %param.11) | copy-start | bytes 1156
  28.0 14.1 %all-to-all-start = ((bf16[16,16,192]{2,1,0:T(8,128)(2,1)}), bf16[16,16,192]{2,1,0:T(8,128)(2,1)S(1)}, u32[]{:S(2)}, u32[]{:S(2)}) async-start(bf16[16,16,192]{2,1,0:T(8,128)(2,1)} %broadcast_in_dim.40), calls=%async_computation | async-start | bytes 262144 | tf_op jit(solution)/shard_map/all_to_all | solution.py:92
  42.8 11.6 %all-to-all-start.1 = ((bf16[4,80,192]{2,1,0:T(8,128)(2,1)}), bf16[4,80,192]{2,1,0:T(8,128)(2,1)S(1)}, u32[]{:S(2)}, u32[]{:S(2)}) async-start(bf16[4,80,192]{2,1,0:T(8,128)(2,1)} %maximum_maximum_fusion), calls=%async_computation.1 | async-start | bytes 327680 | tf_op jit(solution)/shard_map/all_to_all | solution.py:101
  46.7 19.5 %copy-start.4 = (f32[8,256]{1,0:T(8,128)S(1)}, f32[8,256]{1,0:T(8,128)}, u32[]{:S(2)}) copy-start(f32[8,256]{1,0:T(8,128)} %param.17) | copy-start | bytes 24580
  46.7 19.5 %copy-start.8 = (s32[2]{0:T(128)S(1)}, s32[2]{0:T(128)}, u32[]{:S(2)}) copy-start(s32[2]{0:T(128)} %param.12) | copy-start | bytes 28
  46.7 19.7 %copy-start.5 = (f32[8,256]{1,0:T(8,128)S(1)}, f32[8,256]{1,0:T(8,128)}, u32[]{:S(2)}) copy-start(f32[8,256]{1,0:T(8,128)} %param.16) | copy-start | bytes 24580
  56.2 19.3 %all-to-all-start.2 = ((bf16[8,16,512]{2,1,0:T(8,128)(2,1)}), bf16[8,16,512]{2,1,0:T(8,128)(2,1)S(1)}, u32[]{:S(2)}, u32[]{:S(2)}) async-start(bf16[8,16,512]{2,1,0:T(8,128)(2,1)} %pad_maximum_fusion.1), calls=%async_computation.2 | async-start | bytes 262144 | tf_op jit(solution)/shard_map/all_to_all | solution.py:131
  66.6 26.0 %copy-start.6 = (f32[8,1,128]{2,1,0:T(1,128)S(1)}, f32[8,1,128]{2,1,0:T(1,128)}, u32[]{:S(2)}) copy-start(f32[8,1,128]{2,1,0:T(1,128)} %param.18) | copy-start | bytes 12292
  76.1 17.1 %copy-start.7 = (f32[8,1,128]{2,1,0:T(1,128)S(1)}, f32[8,1,128]{2,1,0:T(1,128)}, u32[]{:S(2)}) copy-start(f32[8,1,128]{2,1,0:T(1,128)} %param.19) | copy-start | bytes 12292
  88.6 14.5 %all-to-all-start.4 = ((bf16[4,8,16,512]{3,2,1,0:T(8,128)(2,1)}), bf16[4,8,16,512]{3,2,1,0:T(8,128)(2,1)S(1)}, u32[]{:S(2)}, u32[]{:S(2)}) async-start(bf16[4,8,16,512]{3,2,1,0:T(8,128)(2,1)} %broadcast_in_dim.47), calls=%async_computation.4 | async-start | bytes 1048576 | tf_op jit(solution)/shard_map/all_to_all | solution.py:156
Sparse Core Ops, SparseCore 0:
  27.4 88.2 all-gather.1

commit v6 on v4

--- a/solution.py
+++ b/solution.py
@@ -40,14 +40,16 @@
 ):
     step = pl.program_id(0)
 
+    stat = stat_ref[...]
+    new = sum(projected(x_ref[n], w_ref[:, n], gain_ref[n], stat) for n in range(x_ref.shape[0]))
+
     @pl.when(step == 0)
     def _():
-        acc_ref[...] = jnp.zeros_like(acc_ref)
-
-    stat = stat_ref[...]
-    acc_ref[...] += sum(
-        projected(x_ref[n], w_ref[:, n], gain_ref[n], stat) for n in range(x_ref.shape[0])
-    )
+        acc_ref[...] = new
+
+    @pl.when(step > 0)
+    def _():
+        acc_ref[...] += new
 
     @pl.when(step == pl.num_programs(0) - 1)
     def _():

time: 132 us -> 132 us (level)
  no operation moved by 1% of the time
where the time goes in v6:
time: 132 us; the launch traced here: 131 us
  waiting for transfers between devices  44.7 us (34%)
  blocking collectives  32.4 us (25%)
  starting transfers between devices  25.8 us (20%)
  between operations  13.6 us (10%)
  Pallas kernels  8.61 us (7%)
  other arithmetic  2.49 us (2%)
  local copies, waits for them, and re-layouts  2.42 us (2%)
    all_gather x1, blocking collectives, local(): lax.all_gather(flat, 'mp', axis=0, tiled=True, axis_index_groups=along_y)  20.7 us
    all_gather x1, waiting for transfers between devices, local(): lax.all_gather(by_y, 'mp', axis=0, tiled=True, axis_index_groups=along_z)  12.4 us
    all_to_all x1, blocking collectives, local(): lax.all_to_all(jnp.broadcast_to(scaled, (N_Z, 2 * own, rows)), 'mp', 0, 0...  11.7 us
    all_to_all x1, waiting for transfers between devices, local(): lax.all_to_all(jnp.broadcast_to(low, (N_Y, N_Z, 2 * own, rows)), 'mp', 0,...  10 us
    all_to_all x1, starting transfers between devices, local(): lax.all_to_all(sent, 'mp', 0, 0, axis_index_groups=along_z)  9.99 us
    all_to_all x1, waiting for transfers between devices, local(): lax.all_to_all(sent, 'mp', 0, 0, axis_index_groups=along_z)  8.93 us
    pallas_call x1, Pallas kernels, local(): pl.pallas_call(heads_kernel, grid=(N_Z // 4,), in_specs=[pl.BlockSpec((4,...  8.61 us
    all_to_all x1, starting transfers between devices, local(): lax.all_to_all(jnp.broadcast_to(a_shared, (groups, rank // groups, width)...  7.87 us
  transfers between devices with their start and end apart: 5, of which 5 were waited for; matrix products, arithmetic and copies ran while one was open for 5% of the time, Pallas kernels for 0%

profile of v6, /device:TPU:1, one launch (start us, length us, event | category | flops | bytes accessed | tf_op | source)
XLA Modules:
  0.0 131.1 jit_solution(13401446795805178189)
XLA Ops:
  6.5 20.7 %all_gather.6 = bf16[768,512]{1,0:T(8,128)(2,1)} all-gather(bf16[192,512]{1,0:T(8,128)(2,1)} %bitcast.50), channel_id=1, replica_groups={{0,8,16,24},{1,9,17,25},{2,10,18,26},{3,11,19,27},{4,12,20,28},{5,13,21..., dimensions={0}, use_global_device_ids=true | all-gather | bytes 983040 | tf_op jit(solution)/shard_map/all_gather | solution.py:94
  27.3 0.7 broadcast_in_dim.16
  28.0 7.9 %all-to-all-start = ((bf16[16,16,192]{2,1,0:T(8,128)(2,1)}), bf16[16,16,192]{2,1,0:T(8,128)(2,1)S(1)}, u32[]{:S(2)}, u32[]{:S(2)}) async-start(bf16[16,16,192]{2,1,0:T(8,128)(2,1)} %broadcast_in_dim.16), calls=%async_computation | async-start | bytes 262144 | tf_op jit(solution)/shard_map/all_to_all | solution.py:99
  35.8 0.2 convert_reduce_fusion
  36.1 0.3 fusion.3
  36.3 5.7 %all-to-all-done = bf16[16,16,192]{2,1,0:T(8,128)(2,1)S(1)} async-done(((bf16[16,16,192]{2,1,0:T(8,128)(2,1)}), bf16[16,16,192]{2,1,0:T(8,128)(2,1)S(1)}, u32[]{:S(2)}, u32[]{:S(2)}) %all-to-all-start) | async-done | bytes 98336 | tf_op jit(solution)/shard_map/all_to_all | solution.py:99
  42.1 0.8 maximum_maximum_fusion
  42.8 3.9 %all-to-all-start.1 = ((bf16[4,80,192]{2,1,0:T(8,128)(2,1)}), bf16[4,80,192]{2,1,0:T(8,128)(2,1)S(1)}, u32[]{:S(2)}, u32[]{:S(2)}) async-start(bf16[4,80,192]{2,1,0:T(8,128)(2,1)} %maximum_maximum_fusion), calls=%async_computation.1 | async-start | bytes 327680 | tf_op jit(solution)/shard_map/all_to_all | solution.py:108
  46.8 7.7 %all-to-all-done.1 = bf16[4,80,192]{2,1,0:T(8,128)(2,1)S(1)} async-done(((bf16[4,80,192]{2,1,0:T(8,128)(2,1)}), bf16[4,80,192]{2,1,0:T(8,128)(2,1)S(1)}, u32[]{:S(2)}, u32[]{:S(2)}) %all-to-all-start.1) | async-done | bytes 122912 | tf_op jit(solution)/shard_map/all_to_all | solution.py:108
  54.5 0.1 reshape_squeeze.3
  54.6 0.1 copy.26
  54.7 0.1 reshape.239
  54.8 0.1 multiply_reduce_fusion
  55.0 0.1 reshape.241
  55.1 0.1 concatenate.13
  55.2 0.3 fusion.4
  55.5 0.7 pad_maximum_fusion
  56.2 10.0 %all-to-all-start.2 = ((bf16[8,16,512]{2,1,0:T(8,128)(2,1)}), bf16[8,16,512]{2,1,0:T(8,128)(2,1)S(1)}, u32[]{:S(2)}, u32[]{:S(2)}) async-start(bf16[8,16,512]{2,1,0:T(8,128)(2,1)} %pad_maximum_fusion), calls=%async_computation.2 | async-start | bytes 262144 | tf_op jit(solution)/shard_map/all_to_all | solution.py:138
  66.2 0.2 fusion.15
  66.4 0.2 fusion.13
  66.6 8.9 %all-to-all-done.2 = bf16[8,16,512]{2,1,0:T(8,128)(2,1)S(1)} async-done(((bf16[8,16,512]{2,1,0:T(8,128)(2,1)}), bf16[8,16,512]{2,1,0:T(8,128)(2,1)S(1)}, u32[]{:S(2)}, u32[]{:S(2)}) %all-to-all-start.2) | async-done | bytes 131104 | tf_op jit(solution)/shard_map/all_to_all | solution.py:138
  75.6 0.1 fusion.27
  75.9 0.1 fusion.8
  76.1 11.7 %all_to_all.25 = bf16[8,16,512]{2,1,0:T(8,128)(2,1)S(1)} all-to-all(bf16[8,16,512]{2,1,0:T(8,128)(2,1)S(1)} %broadcast_in_dim.40), channel_id=1, replica_groups={{0,1,2,3,4,5,6,7},{8,9,10,11,12,13,14,15},{16,17,18,19,20,21,22,23},{24..., dimensions={0} | all-to-all | bytes 262144 | tf_op jit(solution)/shard_map/all_to_all | solution.py:160
  87.8 0.8 broadcast_in_dim.41
  88.6 4.0 %all-to-all-start.4 = ((bf16[4,8,16,512]{3,2,1,0:T(8,128)(2,1)}), bf16[4,8,16,512]{3,2,1,0:T(8,128)(2,1)S(1)}, u32[]{:S(2)}, u32[]{:S(2)}) async-start(bf16[4,8,16,512]{3,2,1,0:T(8,128)(2,1)} %broadcast_in_dim.41), calls=%async_computation.4 | async-start | bytes 1048576 | tf_op jit(solution)/shard_map/all_to_all | solution.py:163
  92.6 0.2 fusion.20
  92.8 0.2 fusion.19
  93.0 0.1 copy.28
  93.2 10.0 %all-to-all-done.4 = bf16[4,8,16,512]{3,2,1,0:T(8,128)(2,1)S(1)} async-done(((bf16[4,8,16,512]{3,2,1,0:T(8,128)(2,1)}), bf16[4,8,16,512]{3,2,1,0:T(8,128)(2,1)S(1)}, u32[]{:S(2)}, u32[]{:S(2)}) %all-to-all-start.4) | async-done | bytes 524320 | tf_op jit(solution)/shard_map/all_to_all | solution.py:163
  103.2 12.4 %all-gather.2.cloned.1.call-done = bf16[6144,512]{1,0:T(8,128)(2,1)} async-done(((bf16[768,512]{1,0:T(8,128)(2,1)}), bf16[6144,512]{1,0:T(8,128)(2,1)}) %all-gather.2.cloned.1.call-update) | async-done | bytes 6291472 | tf_op jit(solution)/shard_map/all_gather | solution.py:95
  115.7 8.6 %heads.1 = bf16[512,128]{1,0:T(8,128)(2,1)} custom-call(bf16[8,768,512]{2,1,0:T(8,128)(2,1)} %bitcast.46, bf16[4,8,192,384]{3,2,1,0:T(8,128)(2,1)} %bitcast.47, f32[8,1,768]{2,1,0:T(1,128)S(1)} %reshape.244.gain_ref, f32[2,512]{1,0:T(2,128)S(1)} %pad_maximum_fusion.2.stat_ref, bf16[512,512]{1,0:T(8,128)(2,1)S(1)} %bitcast.43, bf16[128,256]{1,0:T(8,128)(2,1)S(1)} %bitcast.45, ...), custom_call_target="tpu_custom_call" | custom-call | flops 2415919104 | bytes 12582912 | tf_op jit(solution)/shard_map/heads/pallas_call | solution.py:176
  (53 shorter events, 0.6 us)
Async XLA Ops:
  6.5 59.7 %copy-start = (f32[8,256]{1,0:T(8,128)S(1)}, f32[8,256]{1,0:T(8,128)}, u32[]{:S(2)}) copy-start(f32[8,256]{1,0:T(8,128)} %param.16) | copy-start | bytes 24580
  6.5 20.7 %copy-start.3 = (bf16[16,192]{1,0:T(8,128)(2,1)S(1)}, bf16[16,192]{1,0:T(8,128)(2,1)}, u32[]{:S(2)}) copy-start(bf16[16,192]{1,0:T(8,128)(2,1)} %param.14) | copy-start | bytes 18436
  6.5 109.1 %all-gather.2.cloned.1.call-start = ((), (), s32[]{:S(2)}) async-start(), calls=%async_computation.5 | async-start | bytes 7077888 | tf_op jit(solution)/shard_map/all_gather | solution.py:95
  27.3 8.6 %copy-start.2 = (bf16[768,512]{1,0:T(8,128)(2,1)S(1)}, bf16[768,512]{1,0:T(8,128)(2,1)}, u32[]{:S(2)}) copy-start(bf16[768,512]{1,0:T(8,128)(2,1)} %all_gather.6) | copy-start | bytes 2359300
  27.3 14.8 %copy-start.4 = (bf16[192]{0:T(256)(128)(2,1)S(1)}, bf16[192]{0:T(256)(128)(2,1)}, u32[]{:S(2)}) copy-start(bf16[192]{0:T(256)(128)(2,1)} %param.11) | copy-start | bytes 1156
  28.0 14.1 %all-to-all-start = ((bf16[16,16,192]{2,1,0:T(8,128)(2,1)}), bf16[16,16,192]{2,1,0:T(8,128)(2,1)S(1)}, u32[]{:S(2)}, u32[]{:S(2)}) async-start(bf16[16,16,192]{2,1,0:T(8,128)(2,1)} %broadcast_in_dim.16), calls=%async_computation | async-start | bytes 262144 | tf_op jit(solution)/shard_map/all_to_all | solution.py:99
  42.8 11.6 %all-to-all-start.1 = ((bf16[4,80,192]{2,1,0:T(8,128)(2,1)}), bf16[4,80,192]{2,1,0:T(8,128)(2,1)S(1)}, u32[]{:S(2)}, u32[]{:S(2)}) async-start(bf16[4,80,192]{2,1,0:T(8,128)(2,1)} %maximum_maximum_fusion), calls=%async_computation.1 | async-start | bytes 327680 | tf_op jit(solution)/shard_map/all_to_all | solution.py:108
  46.7 19.5 %copy-start.8 = (s32[2]{0:T(128)S(1)}, s32[2]{0:T(128)}, u32[]{:S(2)}) copy-start(s32[2]{0:T(128)} %param.12) | copy-start | bytes 28
  46.7 19.7 %copy-start.5 = (f32[8,256]{1,0:T(8,128)S(1)}, f32[8,256]{1,0:T(8,128)}, u32[]{:S(2)}) copy-start(f32[8,256]{1,0:T(8,128)} %param.17) | copy-start | bytes 24580
  56.2 19.3 %all-to-all-start.2 = ((bf16[8,16,512]{2,1,0:T(8,128)(2,1)}), bf16[8,16,512]{2,1,0:T(8,128)(2,1)S(1)}, u32[]{:S(2)}, u32[]{:S(2)}) async-start(bf16[8,16,512]{2,1,0:T(8,128)(2,1)} %pad_maximum_fusion), calls=%async_computation.2 | async-start | bytes 262144 | tf_op jit(solution)/shard_map/all_to_all | solution.py:138
  66.6 26.0 %copy-start.6 = (f32[8,1,128]{2,1,0:T(1,128)S(1)}, f32[8,1,128]{2,1,0:T(1,128)}, u32[]{:S(2)}) copy-start(f32[8,1,128]{2,1,0:T(1,128)} %param.18) | copy-start | bytes 12292
  66.6 26.2 %copy-start.7 = (f32[8,1,128]{2,1,0:T(1,128)S(1)}, f32[8,1,128]{2,1,0:T(1,128)}, u32[]{:S(2)}) copy-start(f32[8,1,128]{2,1,0:T(1,128)} %param.19) | copy-start | bytes 12292
  87.8 27.9 %copy-start.1 = (bf16[1,128,256]{2,1,0:T(8,128)(2,1)S(1)}, bf16[1,128,256]{2,1,0:T(8,128)(2,1)}, u32[]{:S(2)}) copy-start(bf16[1,128,256]{2,1,0:T(8,128)(2,1)} %param.15) | copy-start | bytes 196612
  88.6 14.6 %all-to-all-start.4 = ((bf16[4,8,16,512]{3,2,1,0:T(8,128)(2,1)}), bf16[4,8,16,512]{3,2,1,0:T(8,128)(2,1)S(1)}, u32[]{:S(2)}, u32[]{:S(2)}) async-start(bf16[4,8,16,512]{3,2,1,0:T(8,128)(2,1)} %broadcast_in_dim.41), calls=%async_computation.4 | async-start | bytes 1048576 | tf_op jit(solution)/shard_map/all_to_all | solution.py:163
Sparse Core Ops, SparseCore 0:
  27.4 88.2 all-gather.1
